TPU v7x, 128 devices: a whole 4x4x4 slice. The times are simulated.
128 devices in a mesh: lat: 8 (over z, core), lon: 16 (over y, x).
Axes of the slice: x: 4, y: 4, z: 4, core: 2. Of those that a mesh axis runs over, the one named last changes fastest.
Arguments:
- increment: float32 [8, 16, 128, 2048], P(None, None, 'lat', 'lon'), may hold values from -6 to 6
- courant: float32 [2, 16, 128, 2048], P(None, None, 'lat', 'lon'), may hold values from -0.6 to 0.6
- spectra: bfloat16 [147456, 8461], P(('lat', 'lon')), may hold values from -6 to 6
- components: bfloat16 [300, 8461], replicated, may hold values from -0.0625 to 0.0625
- jacobian: bfloat16 [128, 300], replicated, may hold values from -0.5 to 0.5
- obs_weight: float32 [300], replicated, may hold values from 0.3 to 3
- tile_target: int32 [147456, 1], P(('lat', 'lon')), may hold values from 0 to 127; in each aligned block of 1152 rows (0 to 1151, 1152 to 2303, ...) at most 18 rows name the same one
- tile_cell: int32 [147456], P(('lat', 'lon')), may hold values from 0 to 2047
Outputs:
- gradient: float32 [8, 16, 128, 2048], P(None, None, 'lat', 'lon')
- departures: bfloat16 [147456, 300], P(('lat', 'lon'))
Inputs may be any that keep to these rules, and one draw needn't show every extreme that they name: `tile_target`: among the rows of one device at most 18 name the same tile, a bound that some block reaches of them.
All inputs are finite; a program needn't handle non-finite values.
Results may differ from a plain program's by a relative error of at most 0.0055.
Values may be sent and summed in bfloat16 or wider, within the bound.
No kernel may reach another device: no remote copies, remote signals or barrier semaphores. Data moves between devices by JAX's collectives and lax.ppermute only.
A program may use at most 128 MiB of HBM per device.

v0:
```python
import functools

import jax
import jax.numpy as jnp
from jax import lax
from jax.experimental import pallas as pl
from jax.experimental.pallas import tpu as pltpu
from jax.sharding import PartitionSpec as P

F32 = jnp.float32
BF16 = jnp.bfloat16
TRACERS, LEVELS, ROWS, COLS = 8, 16, 16, 128
FEATS = TRACERS * LEVELS
STEPS = 4
WIDE = ROWS + 2 * STEPS
CAP = 18
LINES, ACROSS = 8, 3
CELLS = CAP // ACROSS
SPLIT = 64
BLOCK = 1280
EARLY = 2
SEGMENTS = 8
SEG = COLS // SEGMENTS
SEG_WIDE = SEG + 2 * STEPS
GROUPS = WIDE // 4
FIRST = 8
EXT = COLS + 2 * FIRST


def params(mib):
    return pltpu.CompilerParams(vmem_limit_bytes=mib * 1024 * 1024)


def took(us):
    return pl.CostEstimate(flops=int(us * 1.15e9), bytes_accessed=int(us * 1e6), transcendentals=0)


def in_hbm(a):
    return pltpu.with_memory_space_constraint(a, pltpu.HBM)


def nn(a, b):
    return lax.dot_general(a, b, (((1,), (0,)), ((), ())), preferred_element_type=F32)


def nt(a, b):
    return lax.dot_general(a, b, (((1,), (1,)), ((), ())), preferred_element_type=F32)


def iota(shape, dim):
    return lax.broadcasted_iota(jnp.int32, shape, dim)


def flipped(a):
    return a.astype(F32).T


def two_parts(a):
    high = a.astype(BF16)
    return high, (a - high.astype(F32)).astype(BF16)


def ranks(target):
    count = target.shape[1]
    tri = (iota((128, 128), 0) <= iota((128, 128), 1)).astype(F32).astype(BF16)
    carry = jnp.zeros((128, 1), F32)
    found = []
    for at in range(0, count, 128):
        hit = (iota((128, 128), 0) == target[:, at : at + 128]).astype(F32)
        upto = nn(hit.astype(BF16), tri) + carry
        carry = upto[:, 127:128]
        found.append(jnp.sum(hit * upto, axis=0, keepdims=True))
    return (jnp.concatenate(found, axis=1) - 1.0).astype(jnp.int32)


def keyed(target, rank):
    line = rank // ACROSS
    return LINES * target + line, rank - ACROSS * line


def key_hits(key, tiles):
    return (iota((LINES * tiles, key.shape[1]), 0) == key).astype(F32).astype(BF16)


def picked(hits, rest, slot):
    chosen = jnp.broadcast_to((rest == slot).astype(F32), (16, rest.shape[1])).astype(BF16)
    rows, count = hits.shape
    return (hits.reshape(rows // 16, 16, count) * chosen[None]).reshape(rows, count)


def begin_kernel(comps, spec, total):
    found = nn(comps[...], spec[...])

    @pl.when(pl.program_id(0) == 0)
    def _():
        total[...] = found

    @pl.when(pl.program_id(0) > 0)
    def _():
        total[...] += found


def begin(comps, spec_t, steps):
    pcs, count = comps.shape[0], spec_t.shape[1]
    return pl.pallas_call(
        begin_kernel,
        grid=(steps,),
        in_specs=[
            pl.BlockSpec((pcs, BLOCK), lambda i: (0, i)),
            pl.BlockSpec((BLOCK, count), lambda i: (i, 0)),
        ],
        out_specs=pl.BlockSpec((pcs, count), lambda i: (0, 0)),
        out_shape=jax.ShapeDtypeStruct((pcs, count), F32),
        compiler_params=params(20), cost_estimate=took(4.5),
        name="begin",
    )(in_hbm(comps), in_hbm(spec_t))


def project_kernel(channels, done, target, cell, comps, spec, total, jac_t, weight, scores, send, sums):
    step = pl.program_id(0)
    steps = pl.num_programs(0)
    count = target.shape[1]
    tiles = send.shape[0] // LINES
    rest = channels - (pl.cdiv(channels, BLOCK) - 1) * BLOCK

    @pl.when(step == 0)
    def _():
        sums[...] = total[...] + nn(comps[...], spec[...])

    @pl.when(jnp.logical_and(step > 0, step < steps - 1))
    def _():
        sums[...] += nn(comps[...], spec[...])

    @pl.when(step == steps - 1)
    def _():
        found = (sums[...] + nn(comps[:, :rest], spec[:rest, :])).astype(BF16)
        scores[...] = found
        high, low = two_parts(flipped(jac_t[...]) * weight[...])
        values = (nn(high, found) + nn(low, found)).T.astype(BF16)
        rank = ranks(target[...])
        key, line = keyed(target[...], rank)
        hits = key_hits(key, tiles)
        for slot in range(1, ACROSS):
            send[:, slot * 128 : slot * 128 + 128] = nn(picked(hits, line, slot), values).astype(BF16)
        number = cell[...] + 1
        upper = number // SPLIT
        lower = number - upper * SPLIT
        lane = iota((128, count), 0)
        coded = jnp.where(lane == rank, upper, 0) + jnp.where(lane - SPLIT == rank, lower, 0)
        here = (iota((tiles, count), 0) == target[...]).astype(F32).astype(BF16)
        codes = nt(here, coded.astype(F32).astype(BF16)).astype(BF16)
        shape = (LINES * tiles, tiles)
        place = (iota(shape, 0) == LINES * iota(shape, 1) + CELLS).astype(F32).astype(BF16)
        send[:, :128] = (nn(picked(hits, line, 0), values) + nn(place, codes)).astype(BF16)


def project(target, cell, comps, spec_t, total, done, jac_t, weight, tiles):
    pcs, channels = comps.shape
    count = spec_t.shape[1]
    steps = pl.cdiv(channels, BLOCK) - done
    whole = lambda a: pl.BlockSpec(a.shape, lambda i: (0, 0))
    return pl.pallas_call(
        functools.partial(project_kernel, channels, done),
        grid=(steps,),
        in_specs=[
            whole(target),
            whole(cell),
            pl.BlockSpec((pcs, BLOCK), lambda i: (0, i + done)),
            pl.BlockSpec((BLOCK, count), lambda i: (i + done, 0)),
            whole(total),
            whole(jac_t),
            whole(weight),
        ],
        out_specs=[
            pl.BlockSpec((pcs, count), lambda i: (0, 0)),
            pl.BlockSpec((LINES * tiles, ACROSS * 128), lambda i: (0, 0)),
        ],
        out_shape=[
            jax.ShapeDtypeStruct((pcs, count), BF16),
            jax.ShapeDtypeStruct((LINES * tiles, ACROSS * 128), BF16),
        ],
        scratch_shapes=[pltpu.VMEM((pcs, count), F32)],
        compiler_params=params(20), cost_estimate=took(13),
        name="project",
    )(target, cell, in_hbm(comps), in_hbm(spec_t), total, jac_t, weight)


def strided(ref, first, count):
    return jnp.concatenate(
        [ref[pl.ds(first + at * ROWS, 8, stride=ROWS), :] for at in range(0, count, 8)], axis=0
    )


def lat_edges_kernel(inc, wind, turned, low, high):
    def turn(row, carry):
        turned[row] = strided(inc, row, FEATS).T
        return carry

    lax.fori_loop(0, ROWS, turn, 0)
    for at in range(STEPS):
        low[at, :FEATS] = turned[at]
        high[at, :FEATS] = turned[ROWS - STEPS + at]
        low[at, FEATS:] = strided(wind, at, 2 * LEVELS)
        high[at, FEATS:] = strided(wind, ROWS - STEPS + at, 2 * LEVELS)


def lat_edges(inc, wind):
    edge = jax.ShapeDtypeStruct((STEPS, FEATS + 2 * LEVELS, COLS), F32)
    return pl.pallas_call(
        lat_edges_kernel,
        out_shape=[jax.ShapeDtypeStruct((ROWS, COLS, FEATS), F32), edge, edge],
        compiler_params=params(4), cost_estimate=took(1.7),
        name="lat_edges",
    )(inc, wind)


def lon_edges_kernel(turned, wind, south, north, winds, low, high):
    for group in range(GROUPS):
        if group == 0:
            four = [south[at, FEATS:] for at in range(4)]
        elif group == GROUPS - 1:
            four = [north[at, FEATS:] for at in range(4)]
        else:
            four = [strided(wind, 4 * group - 4 + at, 2 * LEVELS) for at in range(4)]
        winds[group] = jnp.concatenate(four, axis=0).T
    for row in range(WIDE + GROUPS):
        place = slice(4 * row, 4 * row + 4)
        if row >= WIDE:
            low[place], high[place] = winds[row - WIDE, :4], winds[row - WIDE, COLS - 4 :]
        elif row < STEPS:
            low[place], high[place] = south[row, :4], south[row, COLS - 4 : COLS]
        elif row >= WIDE - STEPS:
            at = row - WIDE + STEPS
            low[place], high[place] = north[at, :4], north[at, COLS - 4 : COLS]
        else:
            low[place], high[place] = turned[row - STEPS, :4], turned[row - STEPS, COLS - 4 :]


def lon_edges(turned, wind, south, north):
    edge = jax.ShapeDtypeStruct((4 * (WIDE + GROUPS), 128), F32)
    return pl.pallas_call(
        lon_edges_kernel,
        out_shape=[jax.ShapeDtypeStruct((GROUPS, COLS, 128), F32), edge, edge],
        compiler_params=params(4), cost_estimate=took(0.3),
        name="lon_edges",
    )(turned, wind, south, north)


def spread(ext, row, full, west, east, mask):
    ext[row, FIRST - 4 : FIRST] = west * mask
    ext[row, FIRST : FIRST + COLS] = full * mask
    ext[row, FIRST + COLS : FIRST + COLS + 4] = east * mask


def segment(ext, row, col):
    return ext[row, pl.ds(FIRST - STEPS + col, SEGMENTS, stride=SEG), :]


def put_coefs(coefs, row, along, across, col, inside):
    coefs[row, col, 0] = (1.0 - along * along - across * across) * inside
    coefs[row, col, 1] = 0.5 * along * (1.0 + along)
    coefs[row, col, 2] = -0.5 * along * (1.0 - along)
    coefs[row, col, 3] = 0.5 * across * (1.0 + across)
    coefs[row, col, 4] = -0.5 * across * (1.0 - across)


def tangent_row(read, coefs, row, step, done):
    west, here = read(row, step - 1), read(row, step)
    for col in range(step, SEG_WIDE - step):
        east = read(row, col + 1)
        value = coefs[row, col, 0] * here + coefs[row, col, 1] * west + coefs[row, col, 2] * east
        value = value + coefs[row, col, 3] * read(row - 1, col) + coefs[row, col, 4] * read(row + 1, col)
        done(col, value)
        west, here = here, east


def adjoint_row(read, coefs, row, step, done):
    def parts(col):
        here = read(row, col)
        return tuple(coefs[row, col, i] * here for i in range(3))

    west, here = parts(step - 1), parts(step)
    for col in range(step, SEG_WIDE - step):
        east = parts(col + 1)
        value = here[0] + east[1] + west[2]
        value = value + coefs[row + 1, col, 3] * read(row + 1, col) + coefs[row - 1, col, 4] * read(row - 1, col)
        done(col, value)
        west, here = here, east


def sweep(one_row, ext, coefs, now, later, finish):
    source = lambda row, col: segment(ext, row, col)
    buffers = (now, later)
    for step in range(1, STEPS + 1):
        sink = buffers[step % 2]

        def advance(row, carry, source=source, sink=sink, step=step):
            def keep(col, value):
                sink[row, col] = value

            last = lambda col, value: finish(row, col, value)
            one_row(source, coefs, row, step, last if step == STEPS else keep)
            return carry

        lax.fori_loop(step, WIDE - step, advance, 0)
        source = lambda row, col, sink=sink: sink[row, col]


def weigh_kernel(winds, west, east, coefs, ext, spot):
    band = lax.axis_index("lat")
    inside = [(band > 0).astype(F32), (band < lax.axis_size("lat") - 1).astype(F32)]
    lane = iota((128, 256), 1)
    for group in range(GROUPS):
        edge = slice(4 * (WIDE + group), 4 * (WIDE + group) + 4)
        spread(spot, 0, winds[group], west[edge], east[edge], 1.0)
        high, low = two_parts(spot[0])
        mask = inside[0] if group == 0 else inside[1] if group == GROUPS - 1 else 1.0
        for at in range(4):
            row = 4 * group + at
            source = 32 * at + LEVELS * (lane // 128) + lane % LEVELS
            copy = (iota((128, 256), 0) == source).astype(F32).astype(BF16)
            both = (nn(high, copy) + nn(low, copy)) * mask
            ext[0, row], ext[1, row] = both[:, :128], both[:, 128:]

    def weigh(row, carry):
        mask = jnp.where(row < STEPS, inside[0], jnp.where(row >= WIDE - STEPS, inside[1], 1.0))
        for col in range(SEG_WIDE):
            along, across = segment(ext.at[0], row, col), segment(ext.at[1], row, col)
            put_coefs(coefs, row, along, across, col, mask)
        return carry

    lax.fori_loop(0, WIDE, weigh, 0)


def weigh(winds, west, east):
    return pl.pallas_call(
        weigh_kernel,
        out_shape=jax.ShapeDtypeStruct((WIDE, SEG_WIDE, 5, 8, 128), F32),
        scratch_shapes=[pltpu.VMEM((2, WIDE, EXT, 128), F32), pltpu.VMEM((1, EXT, 128), F32)],
        compiler_params=params(6), cost_estimate=took(3.3),
        name="weigh",
    )(winds, west, east)


def tangent_kernel(turned, south, north, west, east, coefs, jac_t, weight, state, changed, ext, now, later):
    band = lax.axis_index("lat")
    inside = [(band > 0).astype(F32), (band < lax.axis_size("lat") - 1).astype(F32)]
    for row in range(WIDE):
        edge = slice(4 * row, 4 * row + 4)
        if row < STEPS:
            spread(ext, row, south[row, :FEATS], west[edge], east[edge], inside[0])
        elif row >= WIDE - STEPS:
            spread(ext, row, north[row - WIDE + STEPS, :FEATS], west[edge], east[edge], inside[1])
        else:
            spread(ext, row, turned[row - STEPS], west[edge], east[edge], 1.0)

    def finish(row, col, value):
        changed[row - STEPS, pl.ds(col - STEPS, SEGMENTS, stride=SEG), :] = value

    sweep(tangent_row, ext, coefs, now, later, finish)
    high, low = two_parts(flipped(jac_t[...]) * weight[...])
    high, low = two_parts(nn(high, jac_t[...]) + nn(low, jac_t[...]))
    for row in range(ROWS):
        full = changed[row].astype(BF16)
        state[row] = full
        changed[row] = nn(full, high) + nn(full, low)


def tangent(turned, south, north, west, east, coefs, jac_t, weight):
    return pl.pallas_call(
        tangent_kernel,
        out_shape=[
            jax.ShapeDtypeStruct((ROWS, COLS, FEATS), BF16),
            jax.ShapeDtypeStruct((ROWS, COLS, FEATS), F32),
        ],
        scratch_shapes=[
            pltpu.VMEM((WIDE, EXT, 128), F32),
            pltpu.VMEM((WIDE, SEG_WIDE, 8, 128), F32),
            pltpu.VMEM((WIDE, SEG_WIDE, 8, 128), F32),
        ],
        compiler_params=params(10), cost_estimate=took(4.8),
        name="tangent",
    )(turned, south, north, west, east, coefs, jac_t, weight)


def slot_codes(got, slot):
    rows = got.shape[0]
    coded = got[:, :128].astype(F32).reshape(rows // LINES, LINES, 128)[:, CELLS : CELLS + 1]
    coded = jnp.broadcast_to(coded, (rows // LINES, LINES, 128)).reshape(rows, 128)
    lane = iota((rows, 128), 1) % SPLIT
    return jnp.where(lane == iota((rows, 128), 0) % LINES * ACROSS + slot, coded, 0.0).astype(BF16)


def code_weights(shape, dim):
    return jnp.where(iota(shape, dim) < SPLIT, float(SPLIT), 1.0).astype(BF16)


def place_of(cells):
    upper = jnp.floor(cells * (1.0 / COLS))
    return upper, cells - upper * COLS


def gather_kernel(got, state, send):
    rows = got.shape[0]
    field = state[...].reshape(ROWS * COLS, FEATS)
    lane = iota((rows, 128), 1).astype(F32)
    none = jnp.zeros((rows, 128), BF16)
    for slot in range(ACROSS):
        cells = nn(slot_codes(got, slot), code_weights((128, 128), 0)) - 1.0
        upper, column = place_of(cells)
        upper = upper.astype(BF16)
        along = (column == lane).astype(F32).astype(BF16)
        hits = jnp.concatenate([jnp.where(upper == jnp.bfloat16(row), along, none) for row in range(ROWS)], axis=1)
        send[:, slot * 128 : slot * 128 + 128] = nn(hits, field).astype(BF16)


def gather(got, state):
    return pl.pallas_call(
        gather_kernel,
        out_shape=jax.ShapeDtypeStruct(got.shape, BF16),
        compiler_params=params(10), cost_estimate=took(3.9),
        name="gather",
    )(got, state)


def scatter_kernel(got, changed, forcing, low, high):
    rows = got.shape[0]
    cells = jnp.concatenate(
        [nt(code_weights((16, 128), 1), slot_codes(got, slot))[:1] - 1.0 for slot in range(ACROSS)], axis=1
    )
    terms = jnp.concatenate([got[:, slot * 128 : slot * 128 + 128] for slot in range(ACROSS)], axis=0)
    terms = jnp.concatenate([terms, jnp.ones(terms.shape, BF16)], axis=1)
    shape = (COLS, ACROSS * rows)
    upper, column = place_of(cells)
    along = (iota(shape, 0).astype(F32) == column).astype(F32).astype(BF16)
    upper = jnp.broadcast_to(upper, shape).astype(BF16)
    none = jnp.zeros(shape, BF16)
    for row in range(ROWS):
        found = nn(jnp.where(upper == jnp.bfloat16(row), along, none), terms)
        full = found[:, :FEATS] - found[:, FEATS:] * changed[row]
        forcing[row] = full
        if row < STEPS:
            low[row] = full.astype(BF16)
        if row >= ROWS - STEPS:
            high[row - ROWS + STEPS] = full.astype(BF16)


def scatter(got, changed):
    edge = jax.ShapeDtypeStruct((STEPS, COLS, FEATS), BF16)
    return pl.pallas_call(
        scatter_kernel,
        out_shape=[jax.ShapeDtypeStruct((ROWS, COLS, FEATS), F32), edge, edge],
        compiler_params=params(10), cost_estimate=took(3.7),
        name="scatter",
    )(got, changed)


def forcing_edges_kernel(forcing, south, north, low, high):
    first, last = [], []
    for row in range(WIDE):
        if row < STEPS:
            full = south[row].astype(F32)
        elif row >= WIDE - STEPS:
            full = north[row - WIDE + STEPS].astype(F32)
        else:
            full = forcing[row - STEPS]
        first.append(full[:4])
        last.append(full[COLS - 4 :])
    low[...] = jnp.concatenate(first, axis=0).astype(BF16)
    high[...] = jnp.concatenate(last, axis=0).astype(BF16)


def forcing_edges(forcing, south, north):
    edge = jax.ShapeDtypeStruct((4 * WIDE, FEATS), BF16)
    return pl.pallas_call(
        forcing_edges_kernel, out_shape=[edge, edge], compiler_params=params(4), cost_estimate=took(0.3), name="forcing_edges"
    )(forcing, south, north)


def adjoint_kernel(inc, coefs, forcing, south, north, west, east, out, ext, back, now, later):
    left, right = west[...].astype(F32), east[...].astype(F32)
    for row in range(WIDE):
        if row < STEPS:
            full = south[row].astype(F32)
        elif row >= WIDE - STEPS:
            full = north[row - WIDE + STEPS].astype(F32)
        else:
            full = forcing[row - STEPS]
        edge = slice(4 * row, 4 * row + 4)
        spread(ext, row, full, left[edge], right[edge], 1.0)

    def finish(row, col, value):
        back[row - STEPS, pl.ds(col - STEPS, SEGMENTS, stride=SEG), :] = value

    sweep(adjoint_row, ext, coefs, now, later, finish)

    def turn(row, carry):
        full = back[row].T
        for at in range(0, FEATS, 8):
            place = pl.ds(at * ROWS + row, 8, stride=ROWS)
            out[place, :] = inc[place, :] - full[at : at + 8]
        return carry

    lax.fori_loop(0, ROWS, turn, 0)


def adjoint(inc, coefs, forcing, south, north, west, east):
    return pl.pallas_call(
        adjoint_kernel,
        out_shape=jax.ShapeDtypeStruct(inc.shape, F32),
        scratch_shapes=[
            pltpu.VMEM((WIDE, EXT, 128), F32),
            pltpu.VMEM((ROWS, COLS, FEATS), F32),
            pltpu.VMEM((WIDE, SEG_WIDE, 8, 128), F32),
            pltpu.VMEM((WIDE, SEG_WIDE, 8, 128), F32),
        ],
        compiler_params=params(10), cost_estimate=took(7),
        name="adjoint",
    )(inc, coefs, forcing, south, north, west, east)


def depart_kernel(target, back, scores, jac_t, weight, out):
    tiles = back.shape[0] // LINES
    pcs, count = scores.shape
    key, rest = keyed(target[...], ranks(target[...]))
    hits = key_hits(key, tiles)
    column = jnp.zeros((FEATS, count), F32)
    for slot in range(ACROSS):
        mine = flipped(back[:, slot * 128 : slot * 128 + 128]).astype(BF16)
        column = column + nn(mine, picked(hits, rest, slot))
    scale = jnp.broadcast_to(weight[...], (128, pcs)).T
    column = column.astype(BF16)
    for at in range(0, count, 128):
        model = nn(jac_t[...], column[:, at : at + 128])
        cut = slice(at, at + 128)
        out[:, cut] = (scale * (scores[:, cut].astype(F32) - model)).astype(BF16)


def depart(target, back, scores, jac_t, weight):
    return pl.pallas_call(
        depart_kernel,
        out_shape=jax.ShapeDtypeStruct(scores.shape, BF16),
        compiler_params=params(10), cost_estimate=took(3.5),
        name="depart",
    )(target, back, scores, jac_t, weight)


def ring(value, axis, move):
    count = lax.axis_size(axis)
    return lax.ppermute(value, axis, [(i, (i + move) % count) for i in range(count)])


def swapped(value):
    tiles = value.shape[0] // LINES
    value = value.reshape(tiles, LINES, value.shape[1])
    value = lax.all_to_all(value, ("lat", "lon"), split_axis=0, concat_axis=0, tiled=True)
    return value.reshape(LINES * tiles, value.shape[2])


def shards(increment, courant, spectra, components, jacobian, obs_weight, tile_target, tile_cell):
    tiles = lax.axis_size("lat") * lax.axis_size("lon")
    count = spectra.shape[0]
    inc = increment.reshape(FEATS * ROWS, COLS)
    wind = courant.reshape(2 * LEVELS * ROWS, COLS)
    target = tile_target.reshape(1, count)
    cell = tile_cell.reshape(1, count)
    jac_t = jacobian.T
    weight = obs_weight.reshape(1, -1)

    turned, low, high = lat_edges(inc, wind)
    south = ring(high, "lat", 1)
    north = ring(low, "lat", -1)
    total = begin(components, spectra.T, EARLY)
    total, south, north = lax.optimization_barrier((total, south, north))
    winds, low, high = lon_edges(turned, wind, south, north)
    west = ring(high, "lon", 1)
    east = ring(low, "lon", -1)
    scores, send = project(target, cell, components, spectra.T, total, EARLY, jac_t, weight, tiles)
    send, west, east = lax.optimization_barrier((send, west, east))
    got = swapped(send)
    coefs = weigh(winds, west, east)
    state, changed = tangent(turned, south, north, west, east, coefs, jac_t, weight)

    send = gather(got, state)
    forcing, low, high = scatter(got, changed)
    south = ring(high, "lat", 1)
    north = ring(low, "lat", -1)
    send, forcing = lax.optimization_barrier((send, forcing))
    back = swapped(send)
    low, winds = lax.optimization_barrier((low, winds))
    coefs = weigh(winds, west, east)
    low, high = forcing_edges(forcing, south, north)
    west = ring(high, "lon", 1)
    east = ring(low, "lon", -1)
    gradient = adjoint(inc, coefs, forcing, south, north, west, east)

    departures = depart(target, back, scores, jac_t, weight)
    return gradient.reshape(increment.shape), departures.T


def solution(mesh):
    placed = (
        P(None, None, "lat", "lon"),
        P(None, None, "lat", "lon"),
        P(("lat", "lon"), None),
        P(),
        P(),
        P(),
        P(("lat", "lon"), None),
        P(("lat", "lon")),
    )
    return jax.shard_map(
        shards,
        mesh=mesh,
        in_specs=placed,
        out_specs=(P(None, None, "lat", "lon"), P(("lat", "lon"), None)),
        check_vma=False,
    )
```

profile of v0, /device:TPU:1, one launch (start us, length us, event | category | flops | bytes accessed | tf_op | source)
XLA Modules:
  0.0 100.4 jit_solution(837673899130173793)
XLA Ops:
  1.6 1.2 %copy-done.2 = f32[8,16,16,128]{3,2,1,0:T(8,128)S(1)} copy-done((f32[8,16,16,128]{3,2,1,0:T(8,128)S(1)}, f32[8,16,16,128]{3,2,1,0:T(8,128)}, u32[]{:S(2)}) %copy-start.2) | copy-done | bytes 1048600
  2.8 1.7 %lat_edges.1 = (f32[16,128,128]{2,1,0:T(8,128)S(1)}, f32[4,160,128]{2,1,0:T(8,128)S(1)}, f32[4,160,128]{2,1,0:T(8,128)S(1)}) custom-call(f32[2048,128]{1,0:T(8,128)S(1)} %bitcast.16, f32[512,128]{1,0:T(8,128)S(1)} %bitcast.14), custom_call_target="tpu_custom_call" | custom-call | flops 1955000064 | bytes 1700000 | tf_op jit(solution)/shard_map/lat_edges/pallas_call | solution.py:209
  4.5 3.0 %collective-permute-start = (f32[4,160,128]{2,1,0:T(8,128)S(1)}, f32[4,160,128]{2,1,0:T(8,128)S(1)}, u32[]{:S(2)}, u32[]{:S(2)}) collective-permute-start(f32[4,160,128]{2,1,0:T(8,128)S(1)} %get-tuple-element.26), channel_id=1, source_target_pairs={{0,16},{16,32},{32,48},{48,64},{64,80},{80,96},{96,112},{112,0},{1... | collective-permute-start | bytes 983048 | tf_op jit(solution)/shard_map/ppermute | solution.py:550
  9.0 4.7 %begin.1.total = f32[300,1152]{1,0:T(8,128)S(1)} custom-call(bf16[300,8461]{1,0:T(8,128)(2,1)} %comps.3, bf16[8461,1152]{1,0:T(8,128)(2,1)} %bitcast.23), custom_call_target="tpu_custom_call" | custom-call | flops 5175000064 | bytes 4500000 | tf_op jit(solution)/shard_map/begin/pallas_call | solution.py:105
  14.3 1.3 %collective-permute-start.2 = (f32[120,128]{1,0:T(8,128)S(1)}, f32[120,128]{1,0:T(8,128)S(1)}, u32[]{:S(2)}, u32[]{:S(2)}) collective-permute-start(f32[120,128]{1,0:T(8,128)S(1)} %get-tuple-element.33), channel_id=1, source_target_pairs={{0,1},{1,2},{2,3},{3,4},{4,5},{5,6},{6,7},{7,8},{8,9},{9,10},{10,1... | collective-permute-start | bytes 184328 | tf_op jit(solution)/shard_map/ppermute | solution.py:550
  15.6 3.8 %collective-permute-start.3 = (f32[120,128]{1,0:T(8,128)S(1)}, f32[120,128]{1,0:T(8,128)S(1)}, u32[]{:S(2)}, u32[]{:S(2)}) collective-permute-start(f32[120,128]{1,0:T(8,128)S(1)} %get-tuple-element.34), channel_id=1, source_target_pairs={{0,15},{1,0},{2,1},{3,2},{4,3},{5,4},{6,5},{7,6},{8,7},{9,8},{10,9... | collective-permute-start | bytes 184328 | tf_op jit(solution)/shard_map/ppermute | solution.py:550
  19.4 13.5 %project.1 = (bf16[300,1152]{1,0:T(8,128)(2,1)S(1)}, bf16[1024,384]{1,0:T(8,128)(2,1)}) custom-call(s32[1,1152]{1,0:T(1,128)S(1)} %bitcast.21, s32[1,1152]{1,0:T(1,128)S(1)} %reshape.36.cell, bf16[300,8461]{1,0:T(8,128)(2,1)} %comps.3, bf16[8461,1152]{1,0:T(8,128)(2,1)} %bitcast.24, f32[300,1152]{1,0:T(8,128)S(1)} %begin.1.total, ...), custom_call_target="tpu_custom_call" | custom-call | flops 14949999616 | bytes 13000000 | tf_op jit(solution)/shard_map/project/pallas_call | solution.py:162
  33.7 6.9 %all-to-all-start = ((bf16[128,8,384]{2,1,0:T(8,128)(2,1)}), bf16[128,8,384]{2,1,0:T(8,128)(2,1)S(1)}, u32[]{:S(2)}, u32[]{:S(2)}) async-start(bf16[128,8,384]{2,1,0:T(8,128)(2,1)} %bitcast.5), calls=%async_computation | async-start | bytes 1572864 | tf_op jit(solution)/shard_map/all_to_all | solution.py:556
  40.7 3.3 %weigh.2.coefs = f32[24,24,5,8,128]{4,3,2,1,0:T(8,128)S(1)} custom-call(f32[6,128,128]{2,1,0:T(8,128)S(1)} %get-tuple-element.41.winds, f32[120,128]{1,0:T(8,128)S(1)} %collective-permute-done.2.west, f32[120,128]{1,0:T(8,128)S(1)} %collective-permute-done.3.east), custom_call_target="tpu_custom_call" | custom-call | flops 3795000064 | bytes 3300000 | tf_op jit(solution)/shard_map/weigh/pallas_call | solution.py:336
  44.0 4.9 %tangent.1 = (bf16[16,128,128]{2,1,0:T(8,128)(2,1)S(1)}, f32[16,128,128]{2,1,0:T(8,128)S(1)}) custom-call(f32[16,128,128]{2,1,0:T(8,128)S(1)} %get-tuple-element.30.turned, f32[4,160,128]{2,1,0:T(8,128)S(1)} %collective-permute-done.south, f32[4,160,128]{2,1,0:T(8,128)S(1)} %collective-permute-done.1.north, f32[120,128]{1,0:T(8,128)S(1)} %collective-permute-done.2.west, ...), custom_call_target="tpu_custom_call" | custom-call | flops 5520000000 | bytes 4800000 | tf_op jit(solution)/shard_map/tangent/pallas_call | solution.py:370
  48.9 1.0 copy-done.13
  50.7 6.5 %all-to-all-done = bf16[128,8,384]{2,1,0:T(8,128)(2,1)S(1)} async-done(((bf16[128,8,384]{2,1,0:T(8,128)(2,1)}), bf16[128,8,384]{2,1,0:T(8,128)(2,1)S(1)}, u32[]{:S(2)}, u32[]{:S(2)}) %all-to-all-start) | async-done | bytes 786464 | tf_op jit(solution)/shard_map/all_to_all | solution.py:556
  57.2 1.2 %copy-done.14 = f32[16,128,128]{2,1,0:T(8,128)S(1)} copy-done((f32[16,128,128]{2,1,0:T(8,128)S(1)}, f32[16,128,128]{2,1,0:T(8,128)}, u32[]{:S(2)}) %copy-start.14) | copy-done | bytes 1048600
  58.5 4.3 %scatter.1 = (f32[16,128,128]{2,1,0:T(8,128)S(1)}, bf16[4,128,128]{2,1,0:T(8,128)(2,1)}, bf16[4,128,128]{2,1,0:T(8,128)(2,1)}) custom-call(bf16[1024,384]{1,0:T(8,128)(2,1)S(1)} %bitcast.12, f32[16,128,128]{2,1,0:T(8,128)S(1)} %copy-done.14), custom_call_target="tpu_custom_call" | custom-call | flops 4255000064 | bytes 3700000 | tf_op jit(solution)/shard_map/scatter/pallas_call | solution.py:450
  62.8 1.3 %collective-permute-start.4 = (bf16[4,128,128]{2,1,0:T(8,128)(2,1)}, bf16[4,128,128]{2,1,0:T(8,128)(2,1)S(1)}, u32[]{:S(2)}, u32[]{:S(2)}) collective-permute-start(bf16[4,128,128]{2,1,0:T(8,128)(2,1)} %get-tuple-element.45), channel_id=1, source_target_pairs={{0,16},{16,32},{32,48},{48,64},{64,80},{80,96},{96,112},{112,0},{1... | collective-permute-start | bytes 393224 | tf_op jit(solution)/shard_map/ppermute | solution.py:550
  64.1 4.8 %gather.1 = bf16[1024,384]{1,0:T(8,128)(2,1)} custom-call(bf16[1024,384]{1,0:T(8,128)(2,1)S(1)} %bitcast.13, bf16[16,128,128]{2,1,0:T(8,128)(2,1)S(1)} %copy-done.16), custom_call_target="tpu_custom_call" | custom-call | flops 4485000192 | bytes 3900000 | tf_op jit(solution)/shard_map/gather/pallas_call | solution.py:418
  68.9 6.1 %all-to-all-start.1 = ((bf16[128,8,384]{2,1,0:T(8,128)(2,1)}), bf16[128,8,384]{2,1,0:T(8,128)(2,1)S(1)}, u32[]{:S(2)}, u32[]{:S(2)}) async-start(bf16[128,8,384]{2,1,0:T(8,128)(2,1)} %bitcast.8), calls=%async_computation.1 | async-start | bytes 1572864 | tf_op jit(solution)/shard_map/all_to_all | solution.py:556
  75.0 1.5 %collective-permute-start.6 = (bf16[96,128]{1,0:T(8,128)(2,1)S(1)}, bf16[96,128]{1,0:T(8,128)(2,1)S(1)}, u32[]{:S(2)}, u32[]{:S(2)}) collective-permute-start(bf16[96,128]{1,0:T(8,128)(2,1)S(1)} %get-tuple-element.46), channel_id=1, source_target_pairs={{0,1},{1,2},{2,3},{3,4},{4,5},{5,6},{6,7},{7,8},{8,9},{9,10},{10,1... | collective-permute-start | bytes 73736 | tf_op jit(solution)/shard_map/ppermute | solution.py:550
  76.5 3.9 %collective-permute-start.7 = (bf16[96,128]{1,0:T(8,128)(2,1)S(1)}, bf16[96,128]{1,0:T(8,128)(2,1)S(1)}, u32[]{:S(2)}, u32[]{:S(2)}) collective-permute-start(bf16[96,128]{1,0:T(8,128)(2,1)S(1)} %get-tuple-element.47), channel_id=1, source_target_pairs={{0,15},{1,0},{2,1},{3,2},{4,3},{5,4},{6,5},{7,6},{8,7},{9,8},{10,9... | collective-permute-start | bytes 73736 | tf_op jit(solution)/shard_map/ppermute | solution.py:550
  82.0 3.3 %weigh.3.coefs = f32[24,24,5,8,128]{4,3,2,1,0:T(8,128)S(1)} custom-call(f32[6,128,128]{2,1,0:T(8,128)S(1)} %copy-done.5, f32[120,128]{1,0:T(8,128)S(1)} %copy-done.9, f32[120,128]{1,0:T(8,128)S(1)} %copy-done.11), custom_call_target="tpu_custom_call" | custom-call | flops 3795000064 | bytes 3300000 | tf_op jit(solution)/shard_map/weigh/pallas_call | solution.py:336
  85.4 3.4 %collective-permute-done.6.west = bf16[96,128]{1,0:T(8,128)(2,1)S(1)} collective-permute-done((bf16[96,128]{1,0:T(8,128)(2,1)S(1)}, bf16[96,128]{1,0:T(8,128)(2,1)S(1)}, u32[]{:S(2)}, u32[]{:S(2)}) %collective-permute-start.6) | collective-permute-done | bytes 24608 | tf_op jit(solution)/shard_map/ppermute | solution.py:550
  88.8 6.9 %adjoint.1 = f32[2048,128]{1,0:T(8,128)} custom-call(f32[2048,128]{1,0:T(8,128)S(1)} %bitcast.17, f32[24,24,5,8,128]{4,3,2,1,0:T(8,128)S(1)} %weigh.3.coefs, f32[16,128,128]{2,1,0:T(8,128)S(1)} %get-tuple-element.44.forcing, bf16[4,128,128]{2,1,0:T(8,128)(2,1)S(1)} %collective-permute-done.4.south, bf16[4,128,128]{2,1,0:T(8,128)(2,1)S(1)} %collective-permute-done.5.north, ...), custom_call_target="tpu_custom_call" | custom-call | flops 8049999872 | bytes 7000000 | tf_op jit(solution)/shard_map/adjoint/pallas_call | solution.py:508
  95.7 1.1 %copy-done.18 = bf16[300,1152]{1,0:T(8,128)(2,1)S(1)} copy-done((bf16[300,1152]{1,0:T(8,128)(2,1)S(1)}, bf16[300,1152]{1,0:T(8,128)(2,1)}, u32[]{:S(2)}) %copy-start.18) | copy-done | bytes 691224
  96.8 3.5 %depart.1 = bf16[300,1152]{1,0:T(8,128)(2,1)} custom-call(s32[1,1152]{1,0:T(1,128)S(1)} %bitcast.22, bf16[1024,384]{1,0:T(8,128)(2,1)S(1)} %bitcast.11, bf16[300,1152]{1,0:T(8,128)(2,1)S(1)} %copy-done.18, bf16[300,128]{1,0:T(8,128)(2,1)S(1)} %bitcast.20, f32[1,300]{1,0:T(1,128)S(1)} %reshape.38.weight), custom_call_target="tpu_custom_call" | custom-call | flops 4024999936 | bytes 3500000 | tf_op jit(solution)/shard_map/depart/pallas_call | solution.py:540
  (48 shorter events, 6.3 us)
Async XLA Ops:
  1.6 1.2 %copy-start.2 = (f32[8,16,16,128]{3,2,1,0:T(8,128)S(1)}, f32[8,16,16,128]{3,2,1,0:T(8,128)}, u32[]{:S(2)}) copy-start(f32[8,16,16,128]{3,2,1,0:T(8,128)} %param.8) | copy-start | bytes 3145732
  4.5 9.2 %collective-permute-start = (f32[4,160,128]{2,1,0:T(8,128)S(1)}, f32[4,160,128]{2,1,0:T(8,128)S(1)}, u32[]{:S(2)}, u32[]{:S(2)}) collective-permute-start(f32[4,160,128]{2,1,0:T(8,128)S(1)} %get-tuple-element.26), channel_id=1, source_target_pairs={{0,16},{16,32},{32,48},{48,64},{64,80},{80,96},{96,112},{112,0},{1... | collective-permute-start | bytes 983048 | tf_op jit(solution)/shard_map/ppermute | solution.py:550
  7.6 6.5 %collective-permute-start.1 = (f32[4,160,128]{2,1,0:T(8,128)S(1)}, f32[4,160,128]{2,1,0:T(8,128)S(1)}, u32[]{:S(2)}, u32[]{:S(2)}) collective-permute-start(f32[4,160,128]{2,1,0:T(8,128)S(1)} %get-tuple-element.27), channel_id=1, source_target_pairs={{0,112},{16,0},{32,16},{48,32},{64,48},{80,64},{96,80},{112,96},{1... | collective-permute-start | bytes 983048 | tf_op jit(solution)/shard_map/ppermute | solution.py:550
  9.0 5.1 %copy-start.1 = (f32[2,16,16,128]{3,2,1,0:T(8,128)S(1)}, f32[2,16,16,128]{3,2,1,0:T(8,128)}, u32[]{:S(2)}) copy-start(f32[2,16,16,128]{3,2,1,0:T(8,128)} %param.9) | copy-start | bytes 786436
  9.0 10.4 %copy-start.6 = (bf16[128,300]{0,1:T(8,128)(2,1)S(1)}, bf16[128,300]{0,1:T(8,128)(2,1)}, u32[]{:S(2)}) copy-start(bf16[128,300]{0,1:T(8,128)(2,1)} %param.12) | copy-start | bytes 230404
  9.0 10.4 %copy-start.12 = (s32[1152,1]{0,1:T(1,128)S(1)}, s32[1152,1]{0,1:T(1,128)}, u32[]{:S(2)}) copy-start(s32[1152,1]{0,1:T(1,128)} %param.14) | copy-start | bytes 13828
  14.3 26.4 %copy-start.4 = (f32[6,128,128]{2,1,0:T(8,128)}, f32[6,128,128]{2,1,0:T(8,128)S(1)}, u32[]{:S(2)}) copy-start(f32[6,128,128]{2,1,0:T(8,128)S(1)} %get-tuple-element.41.winds) | copy-start | bytes 1179652
  14.3 19.4 %collective-permute-start.2 = (f32[120,128]{1,0:T(8,128)S(1)}, f32[120,128]{1,0:T(8,128)S(1)}, u32[]{:S(2)}, u32[]{:S(2)}) collective-permute-start(f32[120,128]{1,0:T(8,128)S(1)} %get-tuple-element.33), channel_id=1, source_target_pairs={{0,1},{1,2},{2,3},{3,4},{4,5},{5,6},{6,7},{7,8},{8,9},{9,10},{10,1... | collective-permute-start | bytes 184328 | tf_op jit(solution)/shard_map/ppermute | solution.py:550
  15.6 18.2 %collective-permute-start.3 = (f32[120,128]{1,0:T(8,128)S(1)}, f32[120,128]{1,0:T(8,128)S(1)}, u32[]{:S(2)}, u32[]{:S(2)}) collective-permute-start(f32[120,128]{1,0:T(8,128)S(1)} %get-tuple-element.34), channel_id=1, source_target_pairs={{0,15},{1,0},{2,1},{3,2},{4,3},{5,4},{6,5},{7,6},{8,7},{9,8},{10,9... | collective-permute-start | bytes 184328 | tf_op jit(solution)/shard_map/ppermute | solution.py:550
  33.7 15.2 %copy-start.8 = (f32[120,128]{1,0:T(8,128)}, f32[120,128]{1,0:T(8,128)S(1)}, u32[]{:S(2)}) copy-start(f32[120,128]{1,0:T(8,128)S(1)} %collective-permute-done.2.west) | copy-start | bytes 184324
  33.7 15.2 %copy-start.10 = (f32[120,128]{1,0:T(8,128)}, f32[120,128]{1,0:T(8,128)S(1)}, u32[]{:S(2)}) copy-start(f32[120,128]{1,0:T(8,128)S(1)} %collective-permute-done.3.east) | copy-start | bytes 184324
  33.7 23.5 %all-to-all-start = ((bf16[128,8,384]{2,1,0:T(8,128)(2,1)}), bf16[128,8,384]{2,1,0:T(8,128)(2,1)S(1)}, u32[]{:S(2)}, u32[]{:S(2)}) async-start(bf16[128,8,384]{2,1,0:T(8,128)(2,1)} %bitcast.5), calls=%async_computation | async-start | bytes 1572864 | tf_op jit(solution)/shard_map/all_to_all | solution.py:556
  48.9 1.0 copy-start.13
  57.2 1.2 %copy-start.14 = (f32[16,128,128]{2,1,0:T(8,128)S(1)}, f32[16,128,128]{2,1,0:T(8,128)}, u32[]{:S(2)}) copy-start(f32[16,128,128]{2,1,0:T(8,128)} %copy-done.13) | copy-start | bytes 3145732
  58.5 5.6 %copy-start.16 = (bf16[16,128,128]{2,1,0:T(8,128)(2,1)S(1)}, bf16[16,128,128]{2,1,0:T(8,128)(2,1)}, u32[]{:S(2)}) copy-start(bf16[16,128,128]{2,1,0:T(8,128)(2,1)} %copy-done.15) | copy-start | bytes 1572868
  62.8 17.5 %copy-start.5 = (f32[6,128,128]{2,1,0:T(8,128)S(1)}, f32[6,128,128]{2,1,0:T(8,128)}, u32[]{:S(2)}) copy-start(f32[6,128,128]{2,1,0:T(8,128)} %copy-done.4) | copy-start | bytes 1179652
  62.8 12.2 %collective-permute-start.4 = (bf16[4,128,128]{2,1,0:T(8,128)(2,1)}, bf16[4,128,128]{2,1,0:T(8,128)(2,1)S(1)}, u32[]{:S(2)}, u32[]{:S(2)}) collective-permute-start(bf16[4,128,128]{2,1,0:T(8,128)(2,1)} %get-tuple-element.45), channel_id=1, source_target_pairs={{0,16},{16,32},{32,48},{48,64},{64,80},{80,96},{96,112},{112,0},{1... | collective-permute-start | bytes 393224 | tf_op jit(solution)/shard_map/ppermute | solution.py:550
  64.1 10.9 %collective-permute-start.5 = (bf16[4,128,128]{2,1,0:T(8,128)(2,1)}, bf16[4,128,128]{2,1,0:T(8,128)(2,1)S(1)}, u32[]{:S(2)}, u32[]{:S(2)}) collective-permute-start(bf16[4,128,128]{2,1,0:T(8,128)(2,1)} %get-tuple-element.40), channel_id=1, source_target_pairs={{0,112},{16,0},{32,16},{48,32},{64,48},{80,64},{96,80},{112,96},{1... | collective-permute-start | bytes 393224 | tf_op jit(solution)/shard_map/ppermute | solution.py:550
  68.9 19.9 %copy-start.3 = (f32[8,16,16,128]{3,2,1,0:T(8,128)S(1)}, f32[8,16,16,128]{3,2,1,0:T(8,128)}, u32[]{:S(2)}) copy-start(f32[8,16,16,128]{3,2,1,0:T(8,128)} %param.8) | copy-start | bytes 3145732
  68.9 26.8 %all-to-all-start.1 = ((bf16[128,8,384]{2,1,0:T(8,128)(2,1)}), bf16[128,8,384]{2,1,0:T(8,128)(2,1)S(1)}, u32[]{:S(2)}, u32[]{:S(2)}) async-start(bf16[128,8,384]{2,1,0:T(8,128)(2,1)} %bitcast.8), calls=%async_computation.1 | async-start | bytes 1572864 | tf_op jit(solution)/shard_map/all_to_all | solution.py:556
  75.0 13.8 %collective-permute-start.6 = (bf16[96,128]{1,0:T(8,128)(2,1)S(1)}, bf16[96,128]{1,0:T(8,128)(2,1)S(1)}, u32[]{:S(2)}, u32[]{:S(2)}) collective-permute-start(bf16[96,128]{1,0:T(8,128)(2,1)S(1)} %get-tuple-element.46), channel_id=1, source_target_pairs={{0,1},{1,2},{2,3},{3,4},{4,5},{5,6},{6,7},{7,8},{8,9},{9,10},{10,1... | collective-permute-start | bytes 73736 | tf_op jit(solution)/shard_map/ppermute | solution.py:550
  76.5 12.3 %collective-permute-start.7 = (bf16[96,128]{1,0:T(8,128)(2,1)S(1)}, bf16[96,128]{1,0:T(8,128)(2,1)S(1)}, u32[]{:S(2)}, u32[]{:S(2)}) collective-permute-start(bf16[96,128]{1,0:T(8,128)(2,1)S(1)} %get-tuple-element.47), channel_id=1, source_target_pairs={{0,15},{1,0},{2,1},{3,2},{4,3},{5,4},{6,5},{7,6},{8,7},{9,8},{10,9... | collective-permute-start | bytes 73736 | tf_op jit(solution)/shard_map/ppermute | solution.py:550
  85.4 10.4 %copy-start.7 = (bf16[128,300]{0,1:T(8,128)(2,1)S(1)}, bf16[128,300]{0,1:T(8,128)(2,1)}, u32[]{:S(2)}) copy-start(bf16[128,300]{0,1:T(8,128)(2,1)} %param.12) | copy-start | bytes 230404
  95.7 1.1 %copy-start.18 = (bf16[300,1152]{1,0:T(8,128)(2,1)S(1)}, bf16[300,1152]{1,0:T(8,128)(2,1)}, u32[]{:S(2)}) copy-start(bf16[300,1152]{1,0:T(8,128)(2,1)} %copy-done.17) | copy-start | bytes 2073604
  (5 other events, 4.3 us)
where the time goes:
time: 101 us; the launch traced here: 100 us
  Pallas kernels  51.3 us (51%)
  starting transfers between devices  27.7 us (27%)
  waiting for transfers between devices  10.3 us (10%)
  local copies, waits for them, and re-layouts  10.2 us (10%)
    ppermute x8, starting transfers between devices, ring(): lax.ppermute(value, axis, [(i, (i + move) % count) for i in range(count)])  14.7 us
    pallas_call x1, Pallas kernels, project(): pl.pallas_call(functools.partial(project_kernel, channels, done), grid=(s...  13.5 us
    all_to_all x2, starting transfers between devices, swapped(): lax.all_to_all(value, ('lat', 'lon'), split_axis=0, concat_axis=0, tiled=...  13 us
    unnamed x38, local copies, waits for them, and re-layouts  8.82 us
    pallas_call x1, Pallas kernels, adjoint(): pl.pallas_call(adjoint_kernel, out_shape=jax.ShapeDtypeStruct(inc.shape,...  6.9 us
    pallas_call x2, Pallas kernels, weigh(): pl.pallas_call(weigh_kernel, out_shape=jax.ShapeDtypeStruct((WIDE, SEG_WI...  6.69 us
    all_to_all x2, waiting for transfers between devices, swapped(): lax.all_to_all(value, ('lat', 'lon'), split_axis=0, concat_axis=0, tiled=...  6.54 us
    pallas_call x1, Pallas kernels, tangent(): pl.pallas_call(tangent_kernel, out_shape=[jax.ShapeDtypeStruct((ROWS, COL...  4.85 us
  transfers between devices with their start and end apart: 10, of which 3 were waited for; matrix products, arithmetic and copies ran while one was open for 1% of the time, Pallas kernels for 41%

commit v1 on v0

--- a/solution.py
+++ b/solution.py
@@ -14,11 +14,12 @@
 STEPS = 4
 WIDE = ROWS + 2 * STEPS
 CAP = 18
-LINES, ACROSS = 8, 3
-CELLS = CAP // ACROSS
+LINES, ACROSS = 4, 5
+CELL_LINE, CELL_SLOT = CAP // ACROSS, CAP % ACROSS
 SPLIT = 64
 BLOCK = 1280
 EARLY = 2
+MANY = 4
 SEGMENTS = 8
 SEG = COLS // SEGMENTS
 SEG_WIDE = SEG + 2 * STEPS
@@ -82,12 +83,6 @@
     return (iota((LINES * tiles, key.shape[1]), 0) == key).astype(F32).astype(BF16)
 
 
-def picked(hits, rest, slot):
-    chosen = jnp.broadcast_to((rest == slot).astype(F32), (16, rest.shape[1])).astype(BF16)
-    rows, count = hits.shape
-    return (hits.reshape(rows // 16, 16, count) * chosen[None]).reshape(rows, count)
-
-
 def begin_kernel(comps, spec, total):
     found = nn(comps[...], spec[...])
 
@@ -120,7 +115,7 @@
     step = pl.program_id(0)
     steps = pl.num_programs(0)
     count = target.shape[1]
-    tiles = send.shape[0] // LINES
+    tiles = send.shape[0]
     rest = channels - (pl.cdiv(channels, BLOCK) - 1) * BLOCK
 
     @pl.when(step == 0)
@@ -135,14 +130,13 @@
     def _():
         found = (sums[...] + nn(comps[:, :rest], spec[:rest, :])).astype(BF16)
         scores[...] = found
-        high, low = two_parts(flipped(jac_t[...]) * weight[...])
-        values = (nn(high, found) + nn(low, found)).T.astype(BF16)
+        high, low = two_parts(flipped(jac_t[...]) * weight[...].reshape(1, -1))
+        values = nn(high, found) + nn(low, found)
         rank = ranks(target[...])
         key, line = keyed(target[...], rank)
-        hits = key_hits(key, tiles)
-        for slot in range(1, ACROSS):
-            send[:, slot * 128 : slot * 128 + 128] = nn(picked(hits, line, slot), values).astype(BF16)
-        number = cell[...] + 1
+        values = jnp.concatenate([jnp.where(line == slot, values, 0.0) for slot in range(ACROSS)], axis=0)
+        packed = nn(key_hits(key, tiles), values.T.astype(BF16))
+        number = cell[...].reshape(1, count) + 1
         upper = number // SPLIT
         lower = number - upper * SPLIT
         lane = iota((128, count), 0)
@@ -150,15 +144,19 @@
         here = (iota((tiles, count), 0) == target[...]).astype(F32).astype(BF16)
         codes = nt(here, coded.astype(F32).astype(BF16)).astype(BF16)
         shape = (LINES * tiles, tiles)
-        place = (iota(shape, 0) == LINES * iota(shape, 1) + CELLS).astype(F32).astype(BF16)
-        send[:, :128] = (nn(picked(hits, line, 0), values) + nn(place, codes)).astype(BF16)
+        place = (iota(shape, 0) == LINES * iota(shape, 1) + CELL_LINE).astype(F32).astype(BF16)
+        codes = nn(place, codes)
+        for slot in range(ACROSS):
+            cut = slice(slot * 128, slot * 128 + 128)
+            full = packed[:, cut] + codes if slot == CELL_SLOT else packed[:, cut]
+            send[:, :, cut] = full.astype(BF16).reshape(tiles, LINES, 128)
 
 
 def project(target, cell, comps, spec_t, total, done, jac_t, weight, tiles):
     pcs, channels = comps.shape
     count = spec_t.shape[1]
     steps = pl.cdiv(channels, BLOCK) - done
-    whole = lambda a: pl.BlockSpec(a.shape, lambda i: (0, 0))
+    whole = lambda a: pl.BlockSpec(a.shape, lambda i: (0,) * a.ndim)
     return pl.pallas_call(
         functools.partial(project_kernel, channels, done),
         grid=(steps,),
@@ -173,11 +171,11 @@
         ],
         out_specs=[
             pl.BlockSpec((pcs, count), lambda i: (0, 0)),
-            pl.BlockSpec((LINES * tiles, ACROSS * 128), lambda i: (0, 0)),
+            pl.BlockSpec((tiles, LINES, ACROSS * 128), lambda i: (0, 0, 0)),
         ],
         out_shape=[
             jax.ShapeDtypeStruct((pcs, count), BF16),
-            jax.ShapeDtypeStruct((LINES * tiles, ACROSS * 128), BF16),
+            jax.ShapeDtypeStruct((tiles, LINES, ACROSS * 128), BF16),
         ],
         scratch_shapes=[pltpu.VMEM((pcs, count), F32)],
         compiler_params=params(20), cost_estimate=took(13),
@@ -209,9 +207,9 @@
     return pl.pallas_call(
         lat_edges_kernel,
         out_shape=[jax.ShapeDtypeStruct((ROWS, COLS, FEATS), F32), edge, edge],
-        compiler_params=params(4), cost_estimate=took(1.7),
+        compiler_params=params(6), cost_estimate=took(1.7),
         name="lat_edges",
-    )(inc, wind)
+    )(in_hbm(inc), in_hbm(wind))
 
 
 def lon_edges_kernel(turned, wind, south, north, winds, low, high):
@@ -358,22 +356,20 @@
         changed[row - STEPS, pl.ds(col - STEPS, SEGMENTS, stride=SEG), :] = value
 
     sweep(tangent_row, ext, coefs, now, later, finish)
-    high, low = two_parts(flipped(jac_t[...]) * weight[...])
+    high, low = two_parts(flipped(jac_t[...]) * weight[...].reshape(1, -1))
     high, low = two_parts(nn(high, jac_t[...]) + nn(low, jac_t[...]))
     for row in range(ROWS):
         full = changed[row].astype(BF16)
         state[row] = full
-        changed[row] = nn(full, high) + nn(full, low)
+    state[ROWS], state[ROWS + 1] = high, low
 
 
 def tangent(turned, south, north, west, east, coefs, jac_t, weight):
     return pl.pallas_call(
         tangent_kernel,
-        out_shape=[
-            jax.ShapeDtypeStruct((ROWS, COLS, FEATS), BF16),
-            jax.ShapeDtypeStruct((ROWS, COLS, FEATS), F32),
-        ],
+        out_shape=jax.ShapeDtypeStruct((ROWS + 2, COLS, FEATS), BF16),
         scratch_shapes=[
+            pltpu.VMEM((ROWS, COLS, FEATS), F32),
             pltpu.VMEM((WIDE, EXT, 128), F32),
             pltpu.VMEM((WIDE, SEG_WIDE, 8, 128), F32),
             pltpu.VMEM((WIDE, SEG_WIDE, 8, 128), F32),
@@ -383,10 +379,15 @@
     )(turned, south, north, west, east, coefs, jac_t, weight)
 
 
+def slot_of(message, slot):
+    cut = message[:, :, slot * 128 : slot * 128 + 128]
+    return cut.reshape(cut.shape[0] * LINES, 128)
+
+
 def slot_codes(got, slot):
-    rows = got.shape[0]
-    coded = got[:, :128].astype(F32).reshape(rows // LINES, LINES, 128)[:, CELLS : CELLS + 1]
-    coded = jnp.broadcast_to(coded, (rows // LINES, LINES, 128)).reshape(rows, 128)
+    rows = got.shape[0] * LINES
+    coded = slot_of(got, CELL_SLOT).astype(F32).reshape(got.shape[0], LINES, 128)[:, CELL_LINE : CELL_LINE + 1]
+    coded = jnp.broadcast_to(coded, (got.shape[0], LINES, 128)).reshape(rows, 128)
     lane = iota((rows, 128), 1) % SPLIT
     return jnp.where(lane == iota((rows, 128), 0) % LINES * ACROSS + slot, coded, 0.0).astype(BF16)
 
@@ -401,8 +402,8 @@
 
 
 def gather_kernel(got, state, send):
-    rows = got.shape[0]
-    field = state[...].reshape(ROWS * COLS, FEATS)
+    rows = got.shape[0] * LINES
+    field = state[:ROWS].reshape(ROWS * COLS, FEATS)
     lane = iota((rows, 128), 1).astype(F32)
     none = jnp.zeros((rows, 128), BF16)
     for slot in range(ACROSS):
@@ -411,7 +412,8 @@
         upper = upper.astype(BF16)
         along = (column == lane).astype(F32).astype(BF16)
         hits = jnp.concatenate([jnp.where(upper == jnp.bfloat16(row), along, none) for row in range(ROWS)], axis=1)
-        send[:, slot * 128 : slot * 128 + 128] = nn(hits, field).astype(BF16)
+        found = nn(hits, field).astype(BF16)
+        send[:, :, slot * 128 : slot * 128 + 128] = found.reshape(got.shape[0], LINES, 128)
 
 
 def gather(got, state):
@@ -423,36 +425,40 @@
     )(got, state)
 
 
-def scatter_kernel(got, changed, forcing, low, high):
-    rows = got.shape[0]
+def scatter_kernel(got, state, forcing, low, high):
+    rows = got.shape[0] * LINES
     cells = jnp.concatenate(
         [nt(code_weights((16, 128), 1), slot_codes(got, slot))[:1] - 1.0 for slot in range(ACROSS)], axis=1
     )
-    terms = jnp.concatenate([got[:, slot * 128 : slot * 128 + 128] for slot in range(ACROSS)], axis=0)
+    terms = jnp.concatenate([slot_of(got, slot) for slot in range(ACROSS)], axis=0)
     terms = jnp.concatenate([terms, jnp.ones(terms.shape, BF16)], axis=1)
     shape = (COLS, ACROSS * rows)
     upper, column = place_of(cells)
     along = (iota(shape, 0).astype(F32) == column).astype(F32).astype(BF16)
     upper = jnp.broadcast_to(upper, shape).astype(BF16)
     none = jnp.zeros(shape, BF16)
-    for row in range(ROWS):
-        found = nn(jnp.where(upper == jnp.bfloat16(row), along, none), terms)
-        full = found[:, :FEATS] - found[:, FEATS:] * changed[row]
-        forcing[row] = full
-        if row < STEPS:
-            low[row] = full.astype(BF16)
-        if row >= ROWS - STEPS:
-            high[row - ROWS + STEPS] = full.astype(BF16)
-
-
-def scatter(got, changed):
+    change = jnp.concatenate([state[ROWS], state[ROWS + 1]], axis=1)
+    for first in range(0, ROWS, MANY):
+        hits = [jnp.where(upper == jnp.bfloat16(first + at), along, none) for at in range(MANY)]
+        found = nn(jnp.concatenate(hits, axis=0), terms)
+        changed = nn(state[first : first + MANY].reshape(MANY * COLS, FEATS), change)
+        changed = changed[:, :FEATS] + changed[:, FEATS:]
+        full = (found[:, :FEATS] - found[:, FEATS:] * changed).reshape(MANY, COLS, FEATS)
+        forcing[first : first + MANY] = full
+        if first == 0:
+            low[...] = full[:STEPS].astype(BF16)
+        if first + MANY == ROWS:
+            high[...] = full[MANY - STEPS :].astype(BF16)
+
+
+def scatter(got, state):
     edge = jax.ShapeDtypeStruct((STEPS, COLS, FEATS), BF16)
     return pl.pallas_call(
         scatter_kernel,
         out_shape=[jax.ShapeDtypeStruct((ROWS, COLS, FEATS), F32), edge, edge],
-        compiler_params=params(10), cost_estimate=took(3.7),
+        compiler_params=params(14), cost_estimate=took(3.7),
         name="scatter",
-    )(got, changed)
+    )(got, state)
 
 
 def forcing_edges_kernel(forcing, south, north, low, high):
@@ -520,15 +526,15 @@
 
 
 def depart_kernel(target, back, scores, jac_t, weight, out):
-    tiles = back.shape[0] // LINES
+    tiles = back.shape[0]
     pcs, count = scores.shape
     key, rest = keyed(target[...], ranks(target[...]))
-    hits = key_hits(key, tiles)
+    sent = jnp.concatenate([flipped(slot_of(back, slot)).astype(BF16) for slot in range(ACROSS)], axis=0)
+    found = nn(sent, key_hits(key, tiles))
     column = jnp.zeros((FEATS, count), F32)
     for slot in range(ACROSS):
-        mine = flipped(back[:, slot * 128 : slot * 128 + 128]).astype(BF16)
-        column = column + nn(mine, picked(hits, rest, slot))
-    scale = jnp.broadcast_to(weight[...], (128, pcs)).T
+        column = jnp.where(rest == slot, found[slot * FEATS : (slot + 1) * FEATS], column)
+    scale = jnp.broadcast_to(weight[...].reshape(1, -1), (128, pcs)).T
     column = column.astype(BF16)
     for at in range(0, count, 128):
         model = nn(jac_t[...], column[:, at : at + 128])
@@ -551,10 +557,7 @@
 
 
 def swapped(value):
-    tiles = value.shape[0] // LINES
-    value = value.reshape(tiles, LINES, value.shape[1])
-    value = lax.all_to_all(value, ("lat", "lon"), split_axis=0, concat_axis=0, tiled=True)
-    return value.reshape(LINES * tiles, value.shape[2])
+    return lax.all_to_all(value, ("lat", "lon"), split_axis=0, concat_axis=0, tiled=True)
 
 
 def shards(increment, courant, spectra, components, jacobian, obs_weight, tile_target, tile_cell):
@@ -563,9 +566,9 @@
     inc = increment.reshape(FEATS * ROWS, COLS)
     wind = courant.reshape(2 * LEVELS * ROWS, COLS)
     target = tile_target.reshape(1, count)
-    cell = tile_cell.reshape(1, count)
+    cell = tile_cell
     jac_t = jacobian.T
-    weight = obs_weight.reshape(1, -1)
+    weight = obs_weight
 
     turned, low, high = lat_edges(inc, wind)
     south = ring(high, "lat", 1)
@@ -579,10 +582,10 @@
     send, west, east = lax.optimization_barrier((send, west, east))
     got = swapped(send)
     coefs = weigh(winds, west, east)
-    state, changed = tangent(turned, south, north, west, east, coefs, jac_t, weight)
+    state = tangent(turned, south, north, west, east, coefs, jac_t, weight)
 
     send = gather(got, state)
-    forcing, low, high = scatter(got, changed)
+    forcing, low, high = scatter(got, state)
     south = ring(high, "lat", 1)
     north = ring(low, "lat", -1)
     send, forcing = lax.optimization_barrier((send, forcing))

time: 101 us -> 93.8 us (0.929)
  local copies, waits for them, and re-layouts: 10.2 us -> 5.54 us
  Pallas kernels: 51.3 us -> 49.8 us
  starting transfers between devices: 27.7 us -> 26.6 us
    unnamed x38 -> x32, local copies, waits for them, and re-layouts: 8.82 us -> 5.54 us
    reshape x2 -> x0, local copies, waits for them, and re-layouts: 1.38 us -> none  [the longest x1 0.7 us: shards(): cell = tile_cell.reshape(1, count)]
    pallas_call x1, Pallas kernels: 1.72 us -> 2.99 us  [lat_edges(): pl.pallas_call(lat_edges_kernel, out_shape=[jax.ShapeDtypeStruct((ROWS, C...]
  transfers between devices with their start and end apart: 10 -> 10, of which waited for: 3 -> 3; matrix products, arithmetic and copies ran while one was open for 1% -> 0% of each run, Pallas kernels for 41% -> 42%
where the time goes in v1:
time: 93.8 us; the launch traced here: 93.3 us
  Pallas kernels  49.8 us (53%)
  starting transfers between devices  26.6 us (28%)
  waiting for transfers between devices  10.6 us (11%)
  local copies, waits for them, and re-layouts  5.54 us (6%)
    ppermute x8, starting transfers between devices, ring(): lax.ppermute(value, axis, [(i, (i + move) % count) for i in range(count)])  14.4 us
    pallas_call x1, Pallas kernels, project(): pl.pallas_call(functools.partial(project_kernel, channels, done), grid=(s...  12.5 us
    all_to_all x2, starting transfers between devices, swapped(): lax.all_to_all(value, ('lat', 'lon'), split_axis=0, concat_axis=0, tiled=...  12.2 us
    pallas_call x1, Pallas kernels, adjoint(): pl.pallas_call(adjoint_kernel, out_shape=jax.ShapeDtypeStruct(inc.shape,...  6.91 us
    pallas_call x2, Pallas kernels, weigh(): pl.pallas_call(weigh_kernel, out_shape=jax.ShapeDtypeStruct((WIDE, SEG_WI...  6.69 us
    all_to_all x2, waiting for transfers between devices, swapped(): lax.all_to_all(value, ('lat', 'lon'), split_axis=0, concat_axis=0, tiled=...  6.62 us
    unnamed x32, local copies, waits for them, and re-layouts  5.54 us
    pallas_call x1, Pallas kernels, begin(): pl.pallas_call(begin_kernel, grid=(steps,), in_specs=[pl.BlockSpec((pcs,...  4.73 us
  transfers between devices with their start and end apart: 10, of which 3 were waited for; matrix products, arithmetic and copies ran while one was open for 0% of the time, Pallas kernels for 42%

profile of v1, /device:TPU:1, one launch (start us, length us, event | category | flops | bytes accessed | tf_op | source)
XLA Modules:
  0.0 93.3 jit_solution(1171746795911117157)
XLA Ops:
  0.6 3.0 %lat_edges.1 = (f32[16,128,128]{2,1,0:T(8,128)S(1)}, f32[4,160,128]{2,1,0:T(8,128)S(1)}, f32[4,160,128]{2,1,0:T(8,128)S(1)}) custom-call(f32[2048,128]{1,0:T(8,128)} %bitcast.9, f32[512,128]{1,0:T(8,128)} %bitcast.7), custom_call_target="tpu_custom_call" | custom-call | flops 1955000064 | bytes 1700000 | tf_op jit(solution)/shard_map/lat_edges/pallas_call | solution.py:207
  3.6 3.0 %collective-permute-start = (f32[4,160,128]{2,1,0:T(8,128)S(1)}, f32[4,160,128]{2,1,0:T(8,128)S(1)}, u32[]{:S(2)}, u32[]{:S(2)}) collective-permute-start(f32[4,160,128]{2,1,0:T(8,128)S(1)} %get-tuple-element.24), channel_id=1, source_target_pairs={{0,16},{16,32},{32,48},{48,64},{64,80},{80,96},{96,112},{112,0},{1... | collective-permute-start | bytes 983048 | tf_op jit(solution)/shard_map/ppermute | solution.py:556
  6.7 4.7 %begin.1.total = f32[300,1152]{1,0:T(8,128)S(1)} custom-call(bf16[300,8461]{1,0:T(8,128)(2,1)} %comps.3, bf16[8461,1152]{1,0:T(8,128)(2,1)} %bitcast.16), custom_call_target="tpu_custom_call" | custom-call | flops 5175000064 | bytes 4500000 | tf_op jit(solution)/shard_map/begin/pallas_call | solution.py:100
  11.5 1.7 %collective-permute-done.1.north = f32[4,160,128]{2,1,0:T(8,128)S(1)} collective-permute-done((f32[4,160,128]{2,1,0:T(8,128)S(1)}, f32[4,160,128]{2,1,0:T(8,128)S(1)}, u32[]{:S(2)}, u32[]{:S(2)}) %collective-permute-start.1) | collective-permute-done | bytes 327712 | tf_op jit(solution)/shard_map/ppermute | solution.py:556
  13.4 1.3 %collective-permute-start.2 = (f32[120,128]{1,0:T(8,128)S(1)}, f32[120,128]{1,0:T(8,128)S(1)}, u32[]{:S(2)}, u32[]{:S(2)}) collective-permute-start(f32[120,128]{1,0:T(8,128)S(1)} %get-tuple-element.31), channel_id=1, source_target_pairs={{0,1},{1,2},{2,3},{3,4},{4,5},{5,6},{6,7},{7,8},{8,9},{9,10},{10,1... | collective-permute-start | bytes 184328 | tf_op jit(solution)/shard_map/ppermute | solution.py:556
  14.6 3.8 %collective-permute-start.3 = (f32[120,128]{1,0:T(8,128)S(1)}, f32[120,128]{1,0:T(8,128)S(1)}, u32[]{:S(2)}, u32[]{:S(2)}) collective-permute-start(f32[120,128]{1,0:T(8,128)S(1)} %get-tuple-element.32), channel_id=1, source_target_pairs={{0,15},{1,0},{2,1},{3,2},{4,3},{5,4},{6,5},{7,6},{8,7},{9,8},{10,9... | collective-permute-start | bytes 184328 | tf_op jit(solution)/shard_map/ppermute | solution.py:556
  18.5 12.5 %project.1 = (bf16[300,1152]{1,0:T(8,128)(2,1)S(1)}, bf16[128,4,640]{2,1,0:T(4,128)(2,1)}) custom-call(s32[1,1152]{1,0:T(1,128)S(1)} %bitcast.14, s32[1152]{0:T(1024)S(1)} %copy-done.8, bf16[300,8461]{1,0:T(8,128)(2,1)} %comps.3, bf16[8461,1152]{1,0:T(8,128)(2,1)} %bitcast.17, f32[300,1152]{1,0:T(8,128)S(1)} %begin.1.total, bf16[300,128]{1,0:T(8,128)(2,1)S(1)} %bitcast.11, ...), custom_call_target="tpu_custom_call" | custom-call | flops 14949999616 | bytes 13000000 | tf_op jit(solution)/shard_map/project/pallas_call | solution.py:160
  31.0 0.8 copy-done.14
  31.9 6.1 %all-to-all-start = ((bf16[128,4,640]{2,1,0:T(4,128)(2,1)}), bf16[128,4,640]{2,1,0:T(4,128)(2,1)S(1)}, u32[]{:S(2)}, u32[]{:S(2)}) async-start(bf16[128,4,640]{2,1,0:T(4,128)(2,1)} %get-tuple-element.33), calls=%async_computation | async-start | bytes 1310720 | tf_op jit(solution)/shard_map/all_to_all | solution.py:560
  38.0 3.3 %weigh.2.coefs = f32[24,24,5,8,128]{4,3,2,1,0:T(8,128)S(1)} custom-call(f32[6,128,128]{2,1,0:T(8,128)S(1)} %get-tuple-element.38.winds, f32[120,128]{1,0:T(8,128)S(1)} %collective-permute-done.2.west, f32[120,128]{1,0:T(8,128)S(1)} %collective-permute-done.3.east), custom_call_target="tpu_custom_call" | custom-call | flops 3795000064 | bytes 3300000 | tf_op jit(solution)/shard_map/weigh/pallas_call | solution.py:334
  41.3 4.4 %tangent.1.state = bf16[18,128,128]{2,1,0:T(8,128)(2,1)S(1)} custom-call(f32[16,128,128]{2,1,0:T(8,128)S(1)} %get-tuple-element.28.turned, f32[4,160,128]{2,1,0:T(8,128)S(1)} %collective-permute-done.south, f32[4,160,128]{2,1,0:T(8,128)S(1)} %collective-permute-done.1.north, f32[120,128]{1,0:T(8,128)S(1)} %collective-permute-done.2.west, ...), custom_call_target="tpu_custom_call" | custom-call | flops 5520000000 | bytes 4800000 | tf_op jit(solution)/shard_map/tangent/pallas_call | solution.py:368
  46.6 6.6 %all-to-all-done.got = bf16[128,4,640]{2,1,0:T(4,128)(2,1)S(1)} async-done(((bf16[128,4,640]{2,1,0:T(4,128)(2,1)}), bf16[128,4,640]{2,1,0:T(4,128)(2,1)S(1)}, u32[]{:S(2)}, u32[]{:S(2)}) %all-to-all-start) | async-done | bytes 655392 | tf_op jit(solution)/shard_map/all_to_all | solution.py:560
  53.2 1.1 %copy-done.12 = bf16[18,128,128]{2,1,0:T(8,128)(2,1)S(1)} copy-done((bf16[18,128,128]{2,1,0:T(8,128)(2,1)S(1)}, bf16[18,128,128]{2,1,0:T(8,128)(2,1)}, u32[]{:S(2)}) %copy-start.12) | copy-done | bytes 589848
  54.3 4.0 %scatter.1 = (f32[16,128,128]{2,1,0:T(8,128)S(1)}, bf16[4,128,128]{2,1,0:T(8,128)(2,1)S(1)}, bf16[4,128,128]{2,1,0:T(8,128)(2,1)}) custom-call(bf16[128,4,640]{2,1,0:T(4,128)(2,1)S(1)} %all-to-all-done.got, bf16[18,128,128]{2,1,0:T(8,128)(2,1)S(1)} %copy-done.12), custom_call_target="tpu_custom_call" | custom-call | flops 4255000064 | bytes 3700000 | tf_op jit(solution)/shard_map/scatter/pallas_call | solution.py:456
  58.3 1.2 %collective-permute-start.4 = (bf16[4,128,128]{2,1,0:T(8,128)(2,1)}, bf16[4,128,128]{2,1,0:T(8,128)(2,1)S(1)}, u32[]{:S(2)}, u32[]{:S(2)}) collective-permute-start(bf16[4,128,128]{2,1,0:T(8,128)(2,1)} %get-tuple-element.41), channel_id=1, source_target_pairs={{0,16},{16,32},{32,48},{48,64},{64,80},{80,96},{96,112},{112,0},{1... | collective-permute-start | bytes 393224 | tf_op jit(solution)/shard_map/ppermute | solution.py:556
  59.5 4.2 %gather.1 = bf16[128,4,640]{2,1,0:T(4,128)(2,1)} custom-call(bf16[128,4,640]{2,1,0:T(4,128)(2,1)S(1)} %all-to-all-done.got, bf16[18,128,128]{2,1,0:T(8,128)(2,1)S(1)} %copy-done.13), custom_call_target="tpu_custom_call" | custom-call | flops 4485000192 | bytes 3900000 | tf_op jit(solution)/shard_map/gather/pallas_call | solution.py:420
  63.8 6.1 %all-to-all-start.1 = ((bf16[128,4,640]{2,1,0:T(4,128)(2,1)}), bf16[128,4,640]{2,1,0:T(4,128)(2,1)S(1)}, u32[]{:S(2)}, u32[]{:S(2)}) async-start(bf16[128,4,640]{2,1,0:T(4,128)(2,1)} %gather.1), calls=%async_computation.1 | async-start | bytes 1310720 | tf_op jit(solution)/shard_map/all_to_all | solution.py:560
  69.9 1.5 %collective-permute-start.6 = (bf16[96,128]{1,0:T(8,128)(2,1)S(1)}, bf16[96,128]{1,0:T(8,128)(2,1)S(1)}, u32[]{:S(2)}, u32[]{:S(2)}) collective-permute-start(bf16[96,128]{1,0:T(8,128)(2,1)S(1)} %get-tuple-element.42), channel_id=1, source_target_pairs={{0,1},{1,2},{2,3},{3,4},{4,5},{5,6},{6,7},{7,8},{8,9},{9,10},{10,1... | collective-permute-start | bytes 73736 | tf_op jit(solution)/shard_map/ppermute | solution.py:556
  71.4 3.6 %collective-permute-start.7 = (bf16[96,128]{1,0:T(8,128)(2,1)S(1)}, bf16[96,128]{1,0:T(8,128)(2,1)S(1)}, u32[]{:S(2)}, u32[]{:S(2)}) collective-permute-start(bf16[96,128]{1,0:T(8,128)(2,1)S(1)} %get-tuple-element.43), channel_id=1, source_target_pairs={{0,15},{1,0},{2,1},{3,2},{4,3},{5,4},{6,5},{7,6},{8,7},{9,8},{10,9... | collective-permute-start | bytes 73736 | tf_op jit(solution)/shard_map/ppermute | solution.py:556
  76.7 3.3 %weigh.3.coefs = f32[24,24,5,8,128]{4,3,2,1,0:T(8,128)S(1)} custom-call(f32[6,128,128]{2,1,0:T(8,128)S(1)} %get-tuple-element.38.winds, f32[120,128]{1,0:T(8,128)S(1)} %copy-done.5, f32[120,128]{1,0:T(8,128)S(1)} %copy-done.7), custom_call_target="tpu_custom_call" | custom-call | flops 3795000064 | bytes 3300000 | tf_op jit(solution)/shard_map/weigh/pallas_call | solution.py:334
  80.0 2.3 %collective-permute-done.6.west = bf16[96,128]{1,0:T(8,128)(2,1)S(1)} collective-permute-done((bf16[96,128]{1,0:T(8,128)(2,1)S(1)}, bf16[96,128]{1,0:T(8,128)(2,1)S(1)}, u32[]{:S(2)}, u32[]{:S(2)}) %collective-permute-start.6) | collective-permute-done | bytes 24608 | tf_op jit(solution)/shard_map/ppermute | solution.py:556
  82.3 6.9 %adjoint.1 = f32[2048,128]{1,0:T(8,128)} custom-call(f32[2048,128]{1,0:T(8,128)S(1)} %bitcast.10, f32[24,24,5,8,128]{4,3,2,1,0:T(8,128)S(1)} %weigh.3.coefs, f32[16,128,128]{2,1,0:T(8,128)S(1)} %get-tuple-element.40.forcing, bf16[4,128,128]{2,1,0:T(8,128)(2,1)S(1)} %collective-permute-done.4.south, bf16[4,128,128]{2,1,0:T(8,128)(2,1)S(1)} %collective-permute-done.5.north, ...), custom_call_target="tpu_custom_call" | custom-call | flops 8049999872 | bytes 7000000 | tf_op jit(solution)/shard_map/adjoint/pallas_call | solution.py:514
  89.2 1.1 %copy-done.15 = bf16[300,1152]{1,0:T(8,128)(2,1)S(1)} copy-done((bf16[300,1152]{1,0:T(8,128)(2,1)S(1)}, bf16[300,1152]{1,0:T(8,128)(2,1)}, u32[]{:S(2)}) %copy-start.15) | copy-done | bytes 691224
  90.3 3.0 %depart.1 = bf16[300,1152]{1,0:T(8,128)(2,1)} custom-call(s32[1,1152]{1,0:T(1,128)S(1)} %bitcast.15, bf16[128,4,640]{2,1,0:T(4,128)(2,1)S(1)} %all-to-all-done.1.back, bf16[300,1152]{1,0:T(8,128)(2,1)S(1)} %copy-done.15, bf16[300,128]{1,0:T(8,128)(2,1)S(1)} %bitcast.13, f32[300]{0:T(512)S(1)} %copy-done.10), custom_call_target="tpu_custom_call" | custom-call | flops 4024999936 | bytes 3500000 | tf_op jit(solution)/shard_map/depart/pallas_call | solution.py:546
  (40 shorter events, 2.8 us)
Async XLA Ops:
  3.6 7.8 %collective-permute-start = (f32[4,160,128]{2,1,0:T(8,128)S(1)}, f32[4,160,128]{2,1,0:T(8,128)S(1)}, u32[]{:S(2)}, u32[]{:S(2)}) collective-permute-start(f32[4,160,128]{2,1,0:T(8,128)S(1)} %get-tuple-element.24), channel_id=1, source_target_pairs={{0,16},{16,32},{32,48},{48,64},{64,80},{80,96},{96,112},{112,0},{1... | collective-permute-start | bytes 983048 | tf_op jit(solution)/shard_map/ppermute | solution.py:556
  6.7 6.5 %collective-permute-start.1 = (f32[4,160,128]{2,1,0:T(8,128)S(1)}, f32[4,160,128]{2,1,0:T(8,128)S(1)}, u32[]{:S(2)}, u32[]{:S(2)}) collective-permute-start(f32[4,160,128]{2,1,0:T(8,128)S(1)} %get-tuple-element.25), channel_id=1, source_target_pairs={{0,112},{16,0},{32,16},{48,32},{64,48},{80,64},{96,80},{112,96},{1... | collective-permute-start | bytes 983048 | tf_op jit(solution)/shard_map/ppermute | solution.py:556
  6.7 6.5 %copy-start = (f32[2,16,16,128]{3,2,1,0:T(8,128)S(1)}, f32[2,16,16,128]{3,2,1,0:T(8,128)}, u32[]{:S(2)}) copy-start(f32[2,16,16,128]{3,2,1,0:T(8,128)} %param.9) | copy-start | bytes 786436
  6.7 11.8 %copy-start.2 = (bf16[128,300]{0,1:T(8,128)(2,1)S(1)}, bf16[128,300]{0,1:T(8,128)(2,1)}, u32[]{:S(2)}) copy-start(bf16[128,300]{0,1:T(8,128)(2,1)} %param.12) | copy-start | bytes 230404
  6.7 11.8 %copy-start.8 = (s32[1152]{0:T(1024)S(1)}, s32[1152]{0:T(1024)}, u32[]{:S(2)}) copy-start(s32[1152]{0:T(1024)} %cell.1) | copy-start | bytes 13828
  6.7 11.8 %copy-start.9 = (s32[1152,1]{0,1:T(1,128)S(1)}, s32[1152,1]{0,1:T(1,128)}, u32[]{:S(2)}) copy-start(s32[1152,1]{0,1:T(1,128)} %param.14) | copy-start | bytes 13828
  6.7 11.8 %copy-start.10 = (f32[300]{0:T(512)S(1)}, f32[300]{0:T(512)}, u32[]{:S(2)}) copy-start(f32[300]{0:T(512)} %weight.5) | copy-start | bytes 3604
  13.4 18.5 %collective-permute-start.2 = (f32[120,128]{1,0:T(8,128)S(1)}, f32[120,128]{1,0:T(8,128)S(1)}, u32[]{:S(2)}, u32[]{:S(2)}) collective-permute-start(f32[120,128]{1,0:T(8,128)S(1)} %get-tuple-element.31), channel_id=1, source_target_pairs={{0,1},{1,2},{2,3},{3,4},{4,5},{5,6},{6,7},{7,8},{8,9},{9,10},{10,1... | collective-permute-start | bytes 184328 | tf_op jit(solution)/shard_map/ppermute | solution.py:556
  14.6 17.2 %collective-permute-start.3 = (f32[120,128]{1,0:T(8,128)S(1)}, f32[120,128]{1,0:T(8,128)S(1)}, u32[]{:S(2)}, u32[]{:S(2)}) collective-permute-start(f32[120,128]{1,0:T(8,128)S(1)} %get-tuple-element.32), channel_id=1, source_target_pairs={{0,15},{1,0},{2,1},{3,2},{4,3},{5,4},{6,5},{7,6},{8,7},{9,8},{10,9... | collective-permute-start | bytes 184328 | tf_op jit(solution)/shard_map/ppermute | solution.py:556
  31.0 0.9 copy-start.14
  31.8 13.9 %copy-start.4 = (f32[120,128]{1,0:T(8,128)}, f32[120,128]{1,0:T(8,128)S(1)}, u32[]{:S(2)}) copy-start(f32[120,128]{1,0:T(8,128)S(1)} %collective-permute-done.2.west) | copy-start | bytes 184324
  31.9 13.9 %copy-start.6 = (f32[120,128]{1,0:T(8,128)}, f32[120,128]{1,0:T(8,128)S(1)}, u32[]{:S(2)}) copy-start(f32[120,128]{1,0:T(8,128)S(1)} %collective-permute-done.3.east) | copy-start | bytes 184324
  31.9 21.4 %all-to-all-start = ((bf16[128,4,640]{2,1,0:T(4,128)(2,1)}), bf16[128,4,640]{2,1,0:T(4,128)(2,1)S(1)}, u32[]{:S(2)}, u32[]{:S(2)}) async-start(bf16[128,4,640]{2,1,0:T(4,128)(2,1)} %get-tuple-element.33), calls=%async_computation | async-start | bytes 1310720 | tf_op jit(solution)/shard_map/all_to_all | solution.py:560
  53.2 1.1 %copy-start.12 = (bf16[18,128,128]{2,1,0:T(8,128)(2,1)S(1)}, bf16[18,128,128]{2,1,0:T(8,128)(2,1)}, u32[]{:S(2)}) copy-start(bf16[18,128,128]{2,1,0:T(8,128)(2,1)} %copy-done.11) | copy-start | bytes 1769476
  54.3 5.2 %copy-start.13 = (bf16[18,128,128]{2,1,0:T(8,128)(2,1)S(1)}, bf16[18,128,128]{2,1,0:T(8,128)(2,1)}, u32[]{:S(2)}) copy-start(bf16[18,128,128]{2,1,0:T(8,128)(2,1)} %copy-done.11) | copy-start | bytes 1769476
  58.3 11.6 %collective-permute-start.4 = (bf16[4,128,128]{2,1,0:T(8,128)(2,1)}, bf16[4,128,128]{2,1,0:T(8,128)(2,1)S(1)}, u32[]{:S(2)}, u32[]{:S(2)}) collective-permute-start(bf16[4,128,128]{2,1,0:T(8,128)(2,1)} %get-tuple-element.41), channel_id=1, source_target_pairs={{0,16},{16,32},{32,48},{48,64},{64,80},{80,96},{96,112},{112,0},{1... | collective-permute-start | bytes 393224 | tf_op jit(solution)/shard_map/ppermute | solution.py:556
  59.5 10.3 %collective-permute-start.5 = (bf16[4,128,128]{2,1,0:T(8,128)(2,1)S(1)}, bf16[4,128,128]{2,1,0:T(8,128)(2,1)S(1)}, u32[]{:S(2)}, u32[]{:S(2)}) collective-permute-start(bf16[4,128,128]{2,1,0:T(8,128)(2,1)S(1)} %get-tuple-element.37), channel_id=1, source_target_pairs={{0,112},{16,0},{32,16},{48,32},{64,48},{80,64},{96,80},{112,96},{1... | collective-permute-start | bytes 393224 | tf_op jit(solution)/shard_map/ppermute | solution.py:556
  63.8 18.5 %copy-start.1 = (f32[8,16,16,128]{3,2,1,0:T(8,128)S(1)}, f32[8,16,16,128]{3,2,1,0:T(8,128)}, u32[]{:S(2)}) copy-start(f32[8,16,16,128]{3,2,1,0:T(8,128)} %param.8) | copy-start | bytes 3145732
  63.8 25.4 %all-to-all-start.1 = ((bf16[128,4,640]{2,1,0:T(4,128)(2,1)}), bf16[128,4,640]{2,1,0:T(4,128)(2,1)S(1)}, u32[]{:S(2)}, u32[]{:S(2)}) async-start(bf16[128,4,640]{2,1,0:T(4,128)(2,1)} %gather.1), calls=%async_computation.1 | async-start | bytes 1310720 | tf_op jit(solution)/shard_map/all_to_all | solution.py:560
  69.9 12.4 %collective-permute-start.6 = (bf16[96,128]{1,0:T(8,128)(2,1)S(1)}, bf16[96,128]{1,0:T(8,128)(2,1)S(1)}, u32[]{:S(2)}, u32[]{:S(2)}) collective-permute-start(bf16[96,128]{1,0:T(8,128)(2,1)S(1)} %get-tuple-element.42), channel_id=1, source_target_pairs={{0,1},{1,2},{2,3},{3,4},{4,5},{5,6},{6,7},{7,8},{8,9},{9,10},{10,1... | collective-permute-start | bytes 73736 | tf_op jit(solution)/shard_map/ppermute | solution.py:556
  71.4 10.9 %collective-permute-start.7 = (bf16[96,128]{1,0:T(8,128)(2,1)S(1)}, bf16[96,128]{1,0:T(8,128)(2,1)S(1)}, u32[]{:S(2)}, u32[]{:S(2)}) collective-permute-start(bf16[96,128]{1,0:T(8,128)(2,1)S(1)} %get-tuple-element.43), channel_id=1, source_target_pairs={{0,15},{1,0},{2,1},{3,2},{4,3},{5,4},{6,5},{7,6},{8,7},{9,8},{10,9... | collective-permute-start | bytes 73736 | tf_op jit(solution)/shard_map/ppermute | solution.py:556
  75.8 0.8 copy-start.7
  80.0 9.2 %copy-start.3 = (bf16[128,300]{0,1:T(8,128)(2,1)S(1)}, bf16[128,300]{0,1:T(8,128)(2,1)}, u32[]{:S(2)}) copy-start(bf16[128,300]{0,1:T(8,128)(2,1)} %param.12) | copy-start | bytes 230404
  89.2 1.1 %copy-start.15 = (bf16[300,1152]{1,0:T(8,128)(2,1)S(1)}, bf16[300,1152]{1,0:T(8,128)(2,1)}, u32[]{:S(2)}) copy-start(bf16[300,1152]{1,0:T(8,128)(2,1)} %copy-done.14) | copy-start | bytes 2073604
  (2 other events, 1.7 us)

commit v2 on v1

--- a/solution.py
+++ b/solution.py
@@ -174,7 +174,7 @@
             pl.BlockSpec((tiles, LINES, ACROSS * 128), lambda i: (0, 0, 0)),
         ],
         out_shape=[
-            jax.ShapeDtypeStruct((pcs, count), BF16),
+            pltpu.HBM((pcs, count), BF16),
             jax.ShapeDtypeStruct((tiles, LINES, ACROSS * 128), BF16),
         ],
         scratch_shapes=[pltpu.VMEM((pcs, count), F32)],
@@ -268,39 +268,44 @@
         east = read(row, col + 1)
         value = coefs[row, col, 0] * here + coefs[row, col, 1] * west + coefs[row, col, 2] * east
         value = value + coefs[row, col, 3] * read(row - 1, col) + coefs[row, col, 4] * read(row + 1, col)
-        done(col, value)
+        done(row, col, value)
         west, here = here, east
 
 
-def adjoint_row(read, coefs, row, step, done):
-    def parts(col):
-        here = read(row, col)
-        return tuple(coefs[row, col, i] * here for i in range(3))
-
-    west, here = parts(step - 1), parts(step)
+def adjoint_rows(read, coefs, row, step, done):
+    def parts(at, col):
+        value = read(row + at, col)
+        return (value,) + tuple(coefs[row + at, col, i] * value for i in range(3))
+
+    west = [parts(at, step - 1) for at in range(2)]
+    here = [parts(at, step) for at in range(2)]
     for col in range(step, SEG_WIDE - step):
-        east = parts(col + 1)
-        value = here[0] + east[1] + west[2]
-        value = value + coefs[row + 1, col, 3] * read(row + 1, col) + coefs[row - 1, col, 4] * read(row - 1, col)
-        done(col, value)
+        east = [parts(at, col + 1) for at in range(2)]
+        below = (read(row - 1, col), here[0][0])
+        above = (here[1][0], read(row + 2, col))
+        for at in range(2):
+            value = here[at][1] + east[at][2] + west[at][3]
+            value = value + coefs[row + at + 1, col, 3] * above[at] + coefs[row + at - 1, col, 4] * below[at]
+            done(row + at, col, value)
         west, here = here, east
 
 
-def sweep(one_row, ext, coefs, now, later, finish):
+def sweep(some_rows, taken, ext, coefs, now, later, finish, after):
     source = lambda row, col: segment(ext, row, col)
     buffers = (now, later)
     for step in range(1, STEPS + 1):
         sink = buffers[step % 2]
 
-        def advance(row, carry, source=source, sink=sink, step=step):
-            def keep(col, value):
+        def advance(turn, carry, source=source, sink=sink, step=step):
+            def keep(row, col, value):
                 sink[row, col] = value
 
-            last = lambda col, value: finish(row, col, value)
-            one_row(source, coefs, row, step, last if step == STEPS else keep)
+            some_rows(source, coefs, step + taken * turn, step, finish if step == STEPS else keep)
+            if step == STEPS:
+                after(turn)
             return carry
 
-        lax.fori_loop(step, WIDE - step, advance, 0)
+        lax.fori_loop(0, (WIDE - 2 * step) // taken, advance, 0)
         source = lambda row, col, sink=sink: sink[row, col]
 
 
@@ -355,7 +360,7 @@
     def finish(row, col, value):
         changed[row - STEPS, pl.ds(col - STEPS, SEGMENTS, stride=SEG), :] = value
 
-    sweep(tangent_row, ext, coefs, now, later, finish)
+    sweep(tangent_row, 1, ext, coefs, now, later, finish, lambda turn: None)
     high, low = two_parts(flipped(jac_t[...]) * weight[...].reshape(1, -1))
     high, low = two_parts(nn(high, jac_t[...]) + nn(low, jac_t[...]))
     for row in range(ROWS):
@@ -498,16 +503,20 @@
     def finish(row, col, value):
         back[row - STEPS, pl.ds(col - STEPS, SEGMENTS, stride=SEG), :] = value
 
-    sweep(adjoint_row, ext, coefs, now, later, finish)
-
-    def turn(row, carry):
+    def turn(row):
         full = back[row].T
         for at in range(0, FEATS, 8):
             place = pl.ds(at * ROWS + row, 8, stride=ROWS)
             out[place, :] = inc[place, :] - full[at : at + 8]
-        return carry
-
-    lax.fori_loop(0, ROWS, turn, 0)
+
+    def behind(pair):
+        first = 2 * jnp.maximum(pair - 1, 0)
+        turn(first)
+        turn(first + 1)
+
+    sweep(adjoint_rows, 2, ext, coefs, now, later, finish, behind)
+    turn(ROWS - 2)
+    turn(ROWS - 1)
 
 
 def adjoint(inc, coefs, forcing, south, north, west, east):

time: 93.8 us -> 91.6 us (0.977)
  Pallas kernels: 49.8 us -> 48.4 us
    pallas_call x1, Pallas kernels: 6.91 us -> 5.31 us  [adjoint(): pl.pallas_call(adjoint_kernel, out_shape=jax.ShapeDtypeStruct(inc.shape,...]
    unnamed x32 -> x30, local copies, waits for them, and re-layouts: 5.54 us -> 4.67 us
where the time goes in v2:
time: 91.6 us; the launch traced here: 91.1 us
  Pallas kernels  48.4 us (53%)
  starting transfers between devices  26.6 us (29%)
  waiting for transfers between devices  10.6 us (12%)
  local copies, waits for them, and re-layouts  4.67 us (5%)
    ppermute x8, starting transfers between devices, ring(): lax.ppermute(value, axis, [(i, (i + move) % count) for i in range(count)])  14.4 us
    pallas_call x1, Pallas kernels, project(): pl.pallas_call(functools.partial(project_kernel, channels, done), grid=(s...  12.8 us
    all_to_all x2, starting transfers between devices, swapped(): lax.all_to_all(value, ('lat', 'lon'), split_axis=0, concat_axis=0, tiled=...  12.2 us
    pallas_call x2, Pallas kernels, weigh(): pl.pallas_call(weigh_kernel, out_shape=jax.ShapeDtypeStruct((WIDE, SEG_WI...  6.68 us
    all_to_all x2, waiting for transfers between devices, swapped(): lax.all_to_all(value, ('lat', 'lon'), split_axis=0, concat_axis=0, tiled=...  6.61 us
    pallas_call x1, Pallas kernels, adjoint(): pl.pallas_call(adjoint_kernel, out_shape=jax.ShapeDtypeStruct(inc.shape,...  5.31 us
    pallas_call x1, Pallas kernels, begin(): pl.pallas_call(begin_kernel, grid=(steps,), in_specs=[pl.BlockSpec((pcs,...  4.73 us
    unnamed x30, local copies, waits for them, and re-layouts  4.67 us
  transfers between devices with their start and end apart: 10, of which 3 were waited for; matrix products, arithmetic and copies ran while one was open for 0% of the time, Pallas kernels for 42%

profile of v2, /device:TPU:1, one launch (start us, length us, event | category | flops | bytes accessed | tf_op | source)
XLA Modules:
  0.0 91.1 jit_solution(4389281293105181245)
XLA Ops:
  0.6 3.0 %lat_edges.1 = (f32[16,128,128]{2,1,0:T(8,128)S(1)}, f32[4,160,128]{2,1,0:T(8,128)S(1)}, f32[4,160,128]{2,1,0:T(8,128)S(1)}) custom-call(f32[2048,128]{1,0:T(8,128)} %bitcast.9, f32[512,128]{1,0:T(8,128)} %bitcast.7), custom_call_target="tpu_custom_call" | custom-call | flops 1955000064 | bytes 1700000 | tf_op jit(solution)/shard_map/lat_edges/pallas_call | solution.py:207
  3.6 3.0 %collective-permute-start = (f32[4,160,128]{2,1,0:T(8,128)S(1)}, f32[4,160,128]{2,1,0:T(8,128)S(1)}, u32[]{:S(2)}, u32[]{:S(2)}) collective-permute-start(f32[4,160,128]{2,1,0:T(8,128)S(1)} %get-tuple-element.24), channel_id=1, source_target_pairs={{0,16},{16,32},{32,48},{48,64},{64,80},{80,96},{96,112},{112,0},{1... | collective-permute-start | bytes 983048 | tf_op jit(solution)/shard_map/ppermute | solution.py:565
  6.7 4.7 %begin.1.total = f32[300,1152]{1,0:T(8,128)S(1)} custom-call(bf16[300,8461]{1,0:T(8,128)(2,1)} %comps.3, bf16[8461,1152]{1,0:T(8,128)(2,1)} %bitcast.16), custom_call_target="tpu_custom_call" | custom-call | flops 5175000064 | bytes 4500000 | tf_op jit(solution)/shard_map/begin/pallas_call | solution.py:100
  11.5 1.7 %collective-permute-done.1.north = f32[4,160,128]{2,1,0:T(8,128)S(1)} collective-permute-done((f32[4,160,128]{2,1,0:T(8,128)S(1)}, f32[4,160,128]{2,1,0:T(8,128)S(1)}, u32[]{:S(2)}, u32[]{:S(2)}) %collective-permute-start.1) | collective-permute-done | bytes 327712 | tf_op jit(solution)/shard_map/ppermute | solution.py:565
  13.4 1.3 %collective-permute-start.2 = (f32[120,128]{1,0:T(8,128)S(1)}, f32[120,128]{1,0:T(8,128)S(1)}, u32[]{:S(2)}, u32[]{:S(2)}) collective-permute-start(f32[120,128]{1,0:T(8,128)S(1)} %get-tuple-element.31), channel_id=1, source_target_pairs={{0,1},{1,2},{2,3},{3,4},{4,5},{5,6},{6,7},{7,8},{8,9},{9,10},{10,1... | collective-permute-start | bytes 184328 | tf_op jit(solution)/shard_map/ppermute | solution.py:565
  14.6 3.8 %collective-permute-start.3 = (f32[120,128]{1,0:T(8,128)S(1)}, f32[120,128]{1,0:T(8,128)S(1)}, u32[]{:S(2)}, u32[]{:S(2)}) collective-permute-start(f32[120,128]{1,0:T(8,128)S(1)} %get-tuple-element.32), channel_id=1, source_target_pairs={{0,15},{1,0},{2,1},{3,2},{4,3},{5,4},{6,5},{7,6},{8,7},{9,8},{10,9... | collective-permute-start | bytes 184328 | tf_op jit(solution)/shard_map/ppermute | solution.py:565
  18.5 12.8 %project.1 = (bf16[300,1152]{1,0:T(8,128)(2,1)}, bf16[128,4,640]{2,1,0:T(4,128)(2,1)}) custom-call(s32[1,1152]{1,0:T(1,128)S(1)} %bitcast.14, s32[1152]{0:T(1024)S(1)} %copy-done.8, bf16[300,8461]{1,0:T(8,128)(2,1)} %comps.3, bf16[8461,1152]{1,0:T(8,128)(2,1)} %bitcast.17, f32[300,1152]{1,0:T(8,128)S(1)} %begin.1.total, bf16[300,128]{1,0:T(8,128)(2,1)S(1)} %bitcast.11, ...), custom_call_target="tpu_custom_call" | custom-call | flops 14949999616 | bytes 13000000 | tf_op jit(solution)/shard_map/project/pallas_call | solution.py:160
  31.2 6.1 %all-to-all-start = ((bf16[128,4,640]{2,1,0:T(4,128)(2,1)}), bf16[128,4,640]{2,1,0:T(4,128)(2,1)S(1)}, u32[]{:S(2)}, u32[]{:S(2)}) async-start(bf16[128,4,640]{2,1,0:T(4,128)(2,1)} %get-tuple-element.33), calls=%async_computation | async-start | bytes 1310720 | tf_op jit(solution)/shard_map/all_to_all | solution.py:569
  37.4 3.3 %weigh.2.coefs = f32[24,24,5,8,128]{4,3,2,1,0:T(8,128)S(1)} custom-call(f32[6,128,128]{2,1,0:T(8,128)S(1)} %get-tuple-element.38.winds, f32[120,128]{1,0:T(8,128)S(1)} %collective-permute-done.2.west, f32[120,128]{1,0:T(8,128)S(1)} %collective-permute-done.3.east), custom_call_target="tpu_custom_call" | custom-call | flops 3795000064 | bytes 3300000 | tf_op jit(solution)/shard_map/weigh/pallas_call | solution.py:339
  40.7 4.4 %tangent.1.state = bf16[18,128,128]{2,1,0:T(8,128)(2,1)S(1)} custom-call(f32[16,128,128]{2,1,0:T(8,128)S(1)} %get-tuple-element.28.turned, f32[4,160,128]{2,1,0:T(8,128)S(1)} %collective-permute-done.south, f32[4,160,128]{2,1,0:T(8,128)S(1)} %collective-permute-done.1.north, f32[120,128]{1,0:T(8,128)S(1)} %collective-permute-done.2.west, ...), custom_call_target="tpu_custom_call" | custom-call | flops 5520000000 | bytes 4800000 | tf_op jit(solution)/shard_map/tangent/pallas_call | solution.py:373
  46.0 6.6 %all-to-all-done.got = bf16[128,4,640]{2,1,0:T(4,128)(2,1)S(1)} async-done(((bf16[128,4,640]{2,1,0:T(4,128)(2,1)}), bf16[128,4,640]{2,1,0:T(4,128)(2,1)S(1)}, u32[]{:S(2)}, u32[]{:S(2)}) %all-to-all-start) | async-done | bytes 655392 | tf_op jit(solution)/shard_map/all_to_all | solution.py:569
  52.6 1.1 %copy-done.12 = bf16[18,128,128]{2,1,0:T(8,128)(2,1)S(1)} copy-done((bf16[18,128,128]{2,1,0:T(8,128)(2,1)S(1)}, bf16[18,128,128]{2,1,0:T(8,128)(2,1)}, u32[]{:S(2)}) %copy-start.12) | copy-done | bytes 589848
  53.7 4.0 %scatter.1 = (f32[16,128,128]{2,1,0:T(8,128)S(1)}, bf16[4,128,128]{2,1,0:T(8,128)(2,1)S(1)}, bf16[4,128,128]{2,1,0:T(8,128)(2,1)}) custom-call(bf16[128,4,640]{2,1,0:T(4,128)(2,1)S(1)} %all-to-all-done.got, bf16[18,128,128]{2,1,0:T(8,128)(2,1)S(1)} %copy-done.12), custom_call_target="tpu_custom_call" | custom-call | flops 4255000064 | bytes 3700000 | tf_op jit(solution)/shard_map/scatter/pallas_call | solution.py:461
  57.7 1.2 %collective-permute-start.4 = (bf16[4,128,128]{2,1,0:T(8,128)(2,1)}, bf16[4,128,128]{2,1,0:T(8,128)(2,1)S(1)}, u32[]{:S(2)}, u32[]{:S(2)}) collective-permute-start(bf16[4,128,128]{2,1,0:T(8,128)(2,1)} %get-tuple-element.41), channel_id=1, source_target_pairs={{0,16},{16,32},{32,48},{48,64},{64,80},{80,96},{96,112},{112,0},{1... | collective-permute-start | bytes 393224 | tf_op jit(solution)/shard_map/ppermute | solution.py:565
  58.9 4.2 %gather.1 = bf16[128,4,640]{2,1,0:T(4,128)(2,1)} custom-call(bf16[128,4,640]{2,1,0:T(4,128)(2,1)S(1)} %all-to-all-done.got, bf16[18,128,128]{2,1,0:T(8,128)(2,1)S(1)} %copy-done.13), custom_call_target="tpu_custom_call" | custom-call | flops 4485000192 | bytes 3900000 | tf_op jit(solution)/shard_map/gather/pallas_call | solution.py:425
  63.2 6.1 %all-to-all-start.1 = ((bf16[128,4,640]{2,1,0:T(4,128)(2,1)}), bf16[128,4,640]{2,1,0:T(4,128)(2,1)S(1)}, u32[]{:S(2)}, u32[]{:S(2)}) async-start(bf16[128,4,640]{2,1,0:T(4,128)(2,1)} %gather.1), calls=%async_computation.1 | async-start | bytes 1310720 | tf_op jit(solution)/shard_map/all_to_all | solution.py:569
  69.3 1.5 %collective-permute-start.6 = (bf16[96,128]{1,0:T(8,128)(2,1)S(1)}, bf16[96,128]{1,0:T(8,128)(2,1)S(1)}, u32[]{:S(2)}, u32[]{:S(2)}) collective-permute-start(bf16[96,128]{1,0:T(8,128)(2,1)S(1)} %get-tuple-element.42), channel_id=1, source_target_pairs={{0,1},{1,2},{2,3},{3,4},{4,5},{5,6},{6,7},{7,8},{8,9},{9,10},{10,1... | collective-permute-start | bytes 73736 | tf_op jit(solution)/shard_map/ppermute | solution.py:565
  70.7 3.6 %collective-permute-start.7 = (bf16[96,128]{1,0:T(8,128)(2,1)S(1)}, bf16[96,128]{1,0:T(8,128)(2,1)S(1)}, u32[]{:S(2)}, u32[]{:S(2)}) collective-permute-start(bf16[96,128]{1,0:T(8,128)(2,1)S(1)} %get-tuple-element.43), channel_id=1, source_target_pairs={{0,15},{1,0},{2,1},{3,2},{4,3},{5,4},{6,5},{7,6},{8,7},{9,8},{10,9... | collective-permute-start | bytes 73736 | tf_op jit(solution)/shard_map/ppermute | solution.py:565
  74.4 0.8 copy-done.5
  76.0 3.3 %weigh.3.coefs = f32[24,24,5,8,128]{4,3,2,1,0:T(8,128)S(1)} custom-call(f32[6,128,128]{2,1,0:T(8,128)S(1)} %get-tuple-element.38.winds, f32[120,128]{1,0:T(8,128)S(1)} %copy-done.5, f32[120,128]{1,0:T(8,128)S(1)} %copy-done.7), custom_call_target="tpu_custom_call" | custom-call | flops 3795000064 | bytes 3300000 | tf_op jit(solution)/shard_map/weigh/pallas_call | solution.py:339
  79.4 2.3 %collective-permute-done.6.west = bf16[96,128]{1,0:T(8,128)(2,1)S(1)} collective-permute-done((bf16[96,128]{1,0:T(8,128)(2,1)S(1)}, bf16[96,128]{1,0:T(8,128)(2,1)S(1)}, u32[]{:S(2)}, u32[]{:S(2)}) %collective-permute-start.6) | collective-permute-done | bytes 24608 | tf_op jit(solution)/shard_map/ppermute | solution.py:565
  81.7 5.3 %adjoint.1 = f32[2048,128]{1,0:T(8,128)} custom-call(f32[2048,128]{1,0:T(8,128)S(1)} %bitcast.10, f32[24,24,5,8,128]{4,3,2,1,0:T(8,128)S(1)} %weigh.3.coefs, f32[16,128,128]{2,1,0:T(8,128)S(1)} %get-tuple-element.40.forcing, bf16[4,128,128]{2,1,0:T(8,128)(2,1)S(1)} %collective-permute-done.4.south, bf16[4,128,128]{2,1,0:T(8,128)(2,1)S(1)} %collective-permute-done.5.north, ...), custom_call_target="tpu_custom_call" | custom-call | flops 8049999872 | bytes 7000000 | tf_op jit(solution)/shard_map/adjoint/pallas_call | solution.py:523
  87.0 1.1 %copy-done.14 = bf16[300,1152]{1,0:T(8,128)(2,1)S(1)} copy-done((bf16[300,1152]{1,0:T(8,128)(2,1)S(1)}, bf16[300,1152]{1,0:T(8,128)(2,1)}, u32[]{:S(2)}) %copy-start.14) | copy-done | bytes 691224
  88.1 3.0 %depart.1 = bf16[300,1152]{1,0:T(8,128)(2,1)} custom-call(s32[1,1152]{1,0:T(1,128)S(1)} %bitcast.15, bf16[128,4,640]{2,1,0:T(4,128)(2,1)S(1)} %all-to-all-done.1.back, bf16[300,1152]{1,0:T(8,128)(2,1)S(1)} %copy-done.14, bf16[300,128]{1,0:T(8,128)(2,1)S(1)} %bitcast.13, f32[300]{0:T(512)S(1)} %copy-done.10), custom_call_target="tpu_custom_call" | custom-call | flops 4024999936 | bytes 3500000 | tf_op jit(solution)/shard_map/depart/pallas_call | solution.py:555
  (38 shorter events, 1.9 us)
Async XLA Ops:
  3.6 7.8 %collective-permute-start = (f32[4,160,128]{2,1,0:T(8,128)S(1)}, f32[4,160,128]{2,1,0:T(8,128)S(1)}, u32[]{:S(2)}, u32[]{:S(2)}) collective-permute-start(f32[4,160,128]{2,1,0:T(8,128)S(1)} %get-tuple-element.24), channel_id=1, source_target_pairs={{0,16},{16,32},{32,48},{48,64},{64,80},{80,96},{96,112},{112,0},{1... | collective-permute-start | bytes 983048 | tf_op jit(solution)/shard_map/ppermute | solution.py:565
  6.7 6.5 %collective-permute-start.1 = (f32[4,160,128]{2,1,0:T(8,128)S(1)}, f32[4,160,128]{2,1,0:T(8,128)S(1)}, u32[]{:S(2)}, u32[]{:S(2)}) collective-permute-start(f32[4,160,128]{2,1,0:T(8,128)S(1)} %get-tuple-element.25), channel_id=1, source_target_pairs={{0,112},{16,0},{32,16},{48,32},{64,48},{80,64},{96,80},{112,96},{1... | collective-permute-start | bytes 983048 | tf_op jit(solution)/shard_map/ppermute | solution.py:565
  6.7 6.5 %copy-start = (f32[2,16,16,128]{3,2,1,0:T(8,128)S(1)}, f32[2,16,16,128]{3,2,1,0:T(8,128)}, u32[]{:S(2)}) copy-start(f32[2,16,16,128]{3,2,1,0:T(8,128)} %param.9) | copy-start | bytes 786436
  6.7 11.8 %copy-start.2 = (bf16[128,300]{0,1:T(8,128)(2,1)S(1)}, bf16[128,300]{0,1:T(8,128)(2,1)}, u32[]{:S(2)}) copy-start(bf16[128,300]{0,1:T(8,128)(2,1)} %param.12) | copy-start | bytes 230404
  6.7 11.8 %copy-start.8 = (s32[1152]{0:T(1024)S(1)}, s32[1152]{0:T(1024)}, u32[]{:S(2)}) copy-start(s32[1152]{0:T(1024)} %cell.1) | copy-start | bytes 13828
  6.7 11.8 %copy-start.9 = (s32[1152,1]{0,1:T(1,128)S(1)}, s32[1152,1]{0,1:T(1,128)}, u32[]{:S(2)}) copy-start(s32[1152,1]{0,1:T(1,128)} %param.14) | copy-start | bytes 13828
  6.7 11.8 %copy-start.10 = (f32[300]{0:T(512)S(1)}, f32[300]{0:T(512)}, u32[]{:S(2)}) copy-start(f32[300]{0:T(512)} %weight.5) | copy-start | bytes 3604
  13.4 17.9 %collective-permute-start.2 = (f32[120,128]{1,0:T(8,128)S(1)}, f32[120,128]{1,0:T(8,128)S(1)}, u32[]{:S(2)}, u32[]{:S(2)}) collective-permute-start(f32[120,128]{1,0:T(8,128)S(1)} %get-tuple-element.31), channel_id=1, source_target_pairs={{0,1},{1,2},{2,3},{3,4},{4,5},{5,6},{6,7},{7,8},{8,9},{9,10},{10,1... | collective-permute-start | bytes 184328 | tf_op jit(solution)/shard_map/ppermute | solution.py:565
  14.6 16.6 %collective-permute-start.3 = (f32[120,128]{1,0:T(8,128)S(1)}, f32[120,128]{1,0:T(8,128)S(1)}, u32[]{:S(2)}, u32[]{:S(2)}) collective-permute-start(f32[120,128]{1,0:T(8,128)S(1)} %get-tuple-element.32), channel_id=1, source_target_pairs={{0,15},{1,0},{2,1},{3,2},{4,3},{5,4},{6,5},{7,6},{8,7},{9,8},{10,9... | collective-permute-start | bytes 184328 | tf_op jit(solution)/shard_map/ppermute | solution.py:565
  31.2 13.9 %copy-start.4 = (f32[120,128]{1,0:T(8,128)}, f32[120,128]{1,0:T(8,128)S(1)}, u32[]{:S(2)}) copy-start(f32[120,128]{1,0:T(8,128)S(1)} %collective-permute-done.2.west) | copy-start | bytes 184324
  31.2 13.9 %copy-start.6 = (f32[120,128]{1,0:T(8,128)}, f32[120,128]{1,0:T(8,128)S(1)}, u32[]{:S(2)}) copy-start(f32[120,128]{1,0:T(8,128)S(1)} %collective-permute-done.3.east) | copy-start | bytes 184324
  31.2 21.4 %all-to-all-start = ((bf16[128,4,640]{2,1,0:T(4,128)(2,1)}), bf16[128,4,640]{2,1,0:T(4,128)(2,1)S(1)}, u32[]{:S(2)}, u32[]{:S(2)}) async-start(bf16[128,4,640]{2,1,0:T(4,128)(2,1)} %get-tuple-element.33), calls=%async_computation | async-start | bytes 1310720 | tf_op jit(solution)/shard_map/all_to_all | solution.py:569
  52.6 1.1 %copy-start.12 = (bf16[18,128,128]{2,1,0:T(8,128)(2,1)S(1)}, bf16[18,128,128]{2,1,0:T(8,128)(2,1)}, u32[]{:S(2)}) copy-start(bf16[18,128,128]{2,1,0:T(8,128)(2,1)} %copy-done.11) | copy-start | bytes 1769476
  53.7 5.2 %copy-start.13 = (bf16[18,128,128]{2,1,0:T(8,128)(2,1)S(1)}, bf16[18,128,128]{2,1,0:T(8,128)(2,1)}, u32[]{:S(2)}) copy-start(bf16[18,128,128]{2,1,0:T(8,128)(2,1)} %copy-done.11) | copy-start | bytes 1769476
  57.7 11.5 %collective-permute-start.4 = (bf16[4,128,128]{2,1,0:T(8,128)(2,1)}, bf16[4,128,128]{2,1,0:T(8,128)(2,1)S(1)}, u32[]{:S(2)}, u32[]{:S(2)}) collective-permute-start(bf16[4,128,128]{2,1,0:T(8,128)(2,1)} %get-tuple-element.41), channel_id=1, source_target_pairs={{0,16},{16,32},{32,48},{48,64},{64,80},{80,96},{96,112},{112,0},{1... | collective-permute-start | bytes 393224 | tf_op jit(solution)/shard_map/ppermute | solution.py:565
  58.9 10.3 %collective-permute-start.5 = (bf16[4,128,128]{2,1,0:T(8,128)(2,1)S(1)}, bf16[4,128,128]{2,1,0:T(8,128)(2,1)S(1)}, u32[]{:S(2)}, u32[]{:S(2)}) collective-permute-start(bf16[4,128,128]{2,1,0:T(8,128)(2,1)S(1)} %get-tuple-element.37), channel_id=1, source_target_pairs={{0,112},{16,0},{32,16},{48,32},{64,48},{80,64},{96,80},{112,96},{1... | collective-permute-start | bytes 393224 | tf_op jit(solution)/shard_map/ppermute | solution.py:565
  63.2 18.5 %copy-start.1 = (f32[8,16,16,128]{3,2,1,0:T(8,128)S(1)}, f32[8,16,16,128]{3,2,1,0:T(8,128)}, u32[]{:S(2)}) copy-start(f32[8,16,16,128]{3,2,1,0:T(8,128)} %param.8) | copy-start | bytes 3145732
  63.2 23.8 %all-to-all-start.1 = ((bf16[128,4,640]{2,1,0:T(4,128)(2,1)}), bf16[128,4,640]{2,1,0:T(4,128)(2,1)S(1)}, u32[]{:S(2)}, u32[]{:S(2)}) async-start(bf16[128,4,640]{2,1,0:T(4,128)(2,1)} %gather.1), calls=%async_computation.1 | async-start | bytes 1310720 | tf_op jit(solution)/shard_map/all_to_all | solution.py:569
  69.3 12.4 %collective-permute-start.6 = (bf16[96,128]{1,0:T(8,128)(2,1)S(1)}, bf16[96,128]{1,0:T(8,128)(2,1)S(1)}, u32[]{:S(2)}, u32[]{:S(2)}) collective-permute-start(bf16[96,128]{1,0:T(8,128)(2,1)S(1)} %get-tuple-element.42), channel_id=1, source_target_pairs={{0,1},{1,2},{2,3},{3,4},{4,5},{5,6},{6,7},{7,8},{8,9},{9,10},{10,1... | collective-permute-start | bytes 73736 | tf_op jit(solution)/shard_map/ppermute | solution.py:565
  70.7 10.9 %collective-permute-start.7 = (bf16[96,128]{1,0:T(8,128)(2,1)S(1)}, bf16[96,128]{1,0:T(8,128)(2,1)S(1)}, u32[]{:S(2)}, u32[]{:S(2)}) collective-permute-start(bf16[96,128]{1,0:T(8,128)(2,1)S(1)} %get-tuple-element.43), channel_id=1, source_target_pairs={{0,15},{1,0},{2,1},{3,2},{4,3},{5,4},{6,5},{7,6},{8,7},{9,8},{10,9... | collective-permute-start | bytes 73736 | tf_op jit(solution)/shard_map/ppermute | solution.py:565
  74.4 0.8 copy-start.5
  75.2 0.8 copy-start.7
  79.4 7.6 %copy-start.3 = (bf16[128,300]{0,1:T(8,128)(2,1)S(1)}, bf16[128,300]{0,1:T(8,128)(2,1)}, u32[]{:S(2)}) copy-start(bf16[128,300]{0,1:T(8,128)(2,1)} %param.12) | copy-start | bytes 230404
  87.0 1.1 %copy-start.14 = (bf16[300,1152]{1,0:T(8,128)(2,1)S(1)}, bf16[300,1152]{1,0:T(8,128)(2,1)}, u32[]{:S(2)}) copy-start(bf16[300,1152]{1,0:T(8,128)(2,1)} %get-tuple-element.45.scores) | copy-start | bytes 2073604
  (1 other events, 0.8 us)

commit v3 on v2

--- a/solution.py
+++ b/solution.py
@@ -16,6 +16,7 @@
 CAP = 18
 LINES, ACROSS = 4, 5
 CELL_LINE, CELL_SLOT = CAP // ACROSS, CAP % ACROSS
+BACK = (2, CAP // 2)
 SPLIT = 64
 BLOCK = 1280
 EARLY = 2
@@ -74,13 +75,13 @@
     return (jnp.concatenate(found, axis=1) - 1.0).astype(jnp.int32)
 
 
-def keyed(target, rank):
-    line = rank // ACROSS
-    return LINES * target + line, rank - ACROSS * line
-
-
-def key_hits(key, tiles):
-    return (iota((LINES * tiles, key.shape[1]), 0) == key).astype(F32).astype(BF16)
+def keyed(target, rank, lines=LINES, across=ACROSS):
+    line = rank // across
+    return lines * target + line, rank - across * line
+
+
+def key_hits(key, rows):
+    return (iota((rows, key.shape[1]), 0) == key).astype(F32).astype(BF16)
 
 
 def begin_kernel(comps, spec, total):
@@ -135,7 +136,7 @@
         rank = ranks(target[...])
         key, line = keyed(target[...], rank)
         values = jnp.concatenate([jnp.where(line == slot, values, 0.0) for slot in range(ACROSS)], axis=0)
-        packed = nn(key_hits(key, tiles), values.T.astype(BF16))
+        packed = nn(key_hits(key, LINES * tiles), values.T.astype(BF16))
         number = cell[...].reshape(1, count) + 1
         upper = number // SPLIT
         lower = number - upper * SPLIT
@@ -386,15 +387,16 @@
 
 def slot_of(message, slot):
     cut = message[:, :, slot * 128 : slot * 128 + 128]
-    return cut.reshape(cut.shape[0] * LINES, 128)
-
-
-def slot_codes(got, slot):
-    rows = got.shape[0] * LINES
-    coded = slot_of(got, CELL_SLOT).astype(F32).reshape(got.shape[0], LINES, 128)[:, CELL_LINE : CELL_LINE + 1]
-    coded = jnp.broadcast_to(coded, (got.shape[0], LINES, 128)).reshape(rows, 128)
+    return cut.reshape(cut.shape[0] * cut.shape[1], 128)
+
+
+def slot_codes(got, slot, lines=LINES, across=ACROSS):
+    tiles = got.shape[0]
+    rows = tiles * lines
+    coded = slot_of(got, CELL_SLOT).astype(F32).reshape(tiles, LINES, 128)[:, CELL_LINE : CELL_LINE + 1]
+    coded = jnp.broadcast_to(coded, (tiles, lines, 128)).reshape(rows, 128)
     lane = iota((rows, 128), 1) % SPLIT
-    return jnp.where(lane == iota((rows, 128), 0) % LINES * ACROSS + slot, coded, 0.0).astype(BF16)
+    return jnp.where(lane == iota((rows, 128), 0) % lines * across + slot, coded, 0.0).astype(BF16)
 
 
 def code_weights(shape, dim):
@@ -407,24 +409,24 @@
 
 
 def gather_kernel(got, state, send):
-    rows = got.shape[0] * LINES
+    rows = got.shape[0] * BACK[0]
     field = state[:ROWS].reshape(ROWS * COLS, FEATS)
     lane = iota((rows, 128), 1).astype(F32)
     none = jnp.zeros((rows, 128), BF16)
-    for slot in range(ACROSS):
-        cells = nn(slot_codes(got, slot), code_weights((128, 128), 0)) - 1.0
+    for slot in range(BACK[1]):
+        cells = nn(slot_codes(got, slot, *BACK), code_weights((128, 128), 0)) - 1.0
         upper, column = place_of(cells)
         upper = upper.astype(BF16)
         along = (column == lane).astype(F32).astype(BF16)
         hits = jnp.concatenate([jnp.where(upper == jnp.bfloat16(row), along, none) for row in range(ROWS)], axis=1)
         found = nn(hits, field).astype(BF16)
-        send[:, :, slot * 128 : slot * 128 + 128] = found.reshape(got.shape[0], LINES, 128)
+        send[:, :, slot * 128 : slot * 128 + 128] = found.reshape(got.shape[0], BACK[0], 128)
 
 
 def gather(got, state):
     return pl.pallas_call(
         gather_kernel,
-        out_shape=jax.ShapeDtypeStruct(got.shape, BF16),
+        out_shape=jax.ShapeDtypeStruct((got.shape[0], BACK[0], BACK[1] * 128), BF16),
         compiler_params=params(10), cost_estimate=took(3.9),
         name="gather",
     )(got, state)
@@ -537,11 +539,11 @@
 def depart_kernel(target, back, scores, jac_t, weight, out):
     tiles = back.shape[0]
     pcs, count = scores.shape
-    key, rest = keyed(target[...], ranks(target[...]))
-    sent = jnp.concatenate([flipped(slot_of(back, slot)).astype(BF16) for slot in range(ACROSS)], axis=0)
-    found = nn(sent, key_hits(key, tiles))
+    key, rest = keyed(target[...], ranks(target[...]), *BACK)
+    sent = jnp.concatenate([flipped(slot_of(back, slot)).astype(BF16) for slot in range(BACK[1])], axis=0)
+    found = nn(sent, key_hits(key, BACK[0] * tiles))
     column = jnp.zeros((FEATS, count), F32)
-    for slot in range(ACROSS):
+    for slot in range(BACK[1]):
         column = jnp.where(rest == slot, found[slot * FEATS : (slot + 1) * FEATS], column)
     scale = jnp.broadcast_to(weight[...].reshape(1, -1), (128, pcs)).T
     column = column.astype(BF16)

time: 91.6 us -> 91.5 us (level)
  transfers between devices with their start and end apart: 10 -> 10, of which waited for: 3 -> 3; matrix products, arithmetic and copies ran while one was open for 0% -> 0% of each run, Pallas kernels for 42% -> 43%
where the time goes in v3:
time: 91.5 us; the launch traced here: 91 us
  Pallas kernels  49 us (54%)
  starting transfers between devices  26.8 us (29%)
  waiting for transfers between devices  9.71 us (11%)
  local copies, waits for them, and re-layouts  4.67 us (5%)
    ppermute x8, starting transfers between devices, ring(): lax.ppermute(value, axis, [(i, (i + move) % count) for i in range(count)])  14.7 us
    pallas_call x1, Pallas kernels, project(): pl.pallas_call(functools.partial(project_kernel, channels, done), grid=(s...  12.8 us
    all_to_all x2, starting transfers between devices, swapped(): lax.all_to_all(value, ('lat', 'lon'), split_axis=0, concat_axis=0, tiled=...  12.2 us
    pallas_call x2, Pallas kernels, weigh(): pl.pallas_call(weigh_kernel, out_shape=jax.ShapeDtypeStruct((WIDE, SEG_WI...  6.69 us
    all_to_all x2, waiting for transfers between devices, swapped(): lax.all_to_all(value, ('lat', 'lon'), split_axis=0, concat_axis=0, tiled=...  6.61 us
    pallas_call x1, Pallas kernels, adjoint(): pl.pallas_call(adjoint_kernel, out_shape=jax.ShapeDtypeStruct(inc.shape,...  5.31 us
    pallas_call x1, Pallas kernels, gather(): pl.pallas_call(gather_kernel, out_shape=jax.ShapeDtypeStruct((got.shape[0...  4.75 us
    pallas_call x1, Pallas kernels, begin(): pl.pallas_call(begin_kernel, grid=(steps,), in_specs=[pl.BlockSpec((pcs,...  4.73 us
  transfers between devices with their start and end apart: 10, of which 3 were waited for; matrix products, arithmetic and copies ran while one was open for 0% of the time, Pallas kernels for 43%

profile of v3, /device:TPU:1, one launch (start us, length us, event | category | flops | bytes accessed | tf_op | source)
XLA Modules:
  0.0 91.0 jit_solution(17246407097932612456)
XLA Ops:
  0.6 3.0 %lat_edges.1 = (f32[16,128,128]{2,1,0:T(8,128)S(1)}, f32[4,160,128]{2,1,0:T(8,128)S(1)}, f32[4,160,128]{2,1,0:T(8,128)S(1)}) custom-call(f32[2048,128]{1,0:T(8,128)} %bitcast.9, f32[512,128]{1,0:T(8,128)} %bitcast.7), custom_call_target="tpu_custom_call" | custom-call | flops 1955000064 | bytes 1700000 | tf_op jit(solution)/shard_map/lat_edges/pallas_call | solution.py:208
  3.6 3.0 %collective-permute-start = (f32[4,160,128]{2,1,0:T(8,128)S(1)}, f32[4,160,128]{2,1,0:T(8,128)S(1)}, u32[]{:S(2)}, u32[]{:S(2)}) collective-permute-start(f32[4,160,128]{2,1,0:T(8,128)S(1)} %get-tuple-element.24), channel_id=1, source_target_pairs={{0,16},{16,32},{32,48},{48,64},{64,80},{80,96},{96,112},{112,0},{1... | collective-permute-start | bytes 983048 | tf_op jit(solution)/shard_map/ppermute | solution.py:567
  6.7 4.7 %begin.1.total = f32[300,1152]{1,0:T(8,128)S(1)} custom-call(bf16[300,8461]{1,0:T(8,128)(2,1)} %comps.3, bf16[8461,1152]{1,0:T(8,128)(2,1)} %bitcast.16), custom_call_target="tpu_custom_call" | custom-call | flops 5175000064 | bytes 4500000 | tf_op jit(solution)/shard_map/begin/pallas_call | solution.py:101
  11.5 1.7 %collective-permute-done.1.north = f32[4,160,128]{2,1,0:T(8,128)S(1)} collective-permute-done((f32[4,160,128]{2,1,0:T(8,128)S(1)}, f32[4,160,128]{2,1,0:T(8,128)S(1)}, u32[]{:S(2)}, u32[]{:S(2)}) %collective-permute-start.1) | collective-permute-done | bytes 327712 | tf_op jit(solution)/shard_map/ppermute | solution.py:567
  13.4 1.3 %collective-permute-start.2 = (f32[120,128]{1,0:T(8,128)S(1)}, f32[120,128]{1,0:T(8,128)S(1)}, u32[]{:S(2)}, u32[]{:S(2)}) collective-permute-start(f32[120,128]{1,0:T(8,128)S(1)} %get-tuple-element.31), channel_id=1, source_target_pairs={{0,1},{1,2},{2,3},{3,4},{4,5},{5,6},{6,7},{7,8},{8,9},{9,10},{10,1... | collective-permute-start | bytes 184328 | tf_op jit(solution)/shard_map/ppermute | solution.py:567
  14.6 3.8 %collective-permute-start.3 = (f32[120,128]{1,0:T(8,128)S(1)}, f32[120,128]{1,0:T(8,128)S(1)}, u32[]{:S(2)}, u32[]{:S(2)}) collective-permute-start(f32[120,128]{1,0:T(8,128)S(1)} %get-tuple-element.32), channel_id=1, source_target_pairs={{0,15},{1,0},{2,1},{3,2},{4,3},{5,4},{6,5},{7,6},{8,7},{9,8},{10,9... | collective-permute-start | bytes 184328 | tf_op jit(solution)/shard_map/ppermute | solution.py:567
  18.5 12.8 %project.1 = (bf16[300,1152]{1,0:T(8,128)(2,1)}, bf16[128,4,640]{2,1,0:T(4,128)(2,1)}) custom-call(s32[1,1152]{1,0:T(1,128)S(1)} %bitcast.14, s32[1152]{0:T(1024)S(1)} %copy-done.8, bf16[300,8461]{1,0:T(8,128)(2,1)} %comps.3, bf16[8461,1152]{1,0:T(8,128)(2,1)} %bitcast.17, f32[300,1152]{1,0:T(8,128)S(1)} %begin.1.total, bf16[300,128]{1,0:T(8,128)(2,1)S(1)} %bitcast.11, ...), custom_call_target="tpu_custom_call" | custom-call | flops 14949999616 | bytes 13000000 | tf_op jit(solution)/shard_map/project/pallas_call | solution.py:161
  31.2 6.1 %all-to-all-start = ((bf16[128,4,640]{2,1,0:T(4,128)(2,1)}), bf16[128,4,640]{2,1,0:T(4,128)(2,1)S(1)}, u32[]{:S(2)}, u32[]{:S(2)}) async-start(bf16[128,4,640]{2,1,0:T(4,128)(2,1)} %get-tuple-element.33), calls=%async_computation | async-start | bytes 1310720 | tf_op jit(solution)/shard_map/all_to_all | solution.py:571
  37.4 3.3 %weigh.2.coefs = f32[24,24,5,8,128]{4,3,2,1,0:T(8,128)S(1)} custom-call(f32[6,128,128]{2,1,0:T(8,128)S(1)} %get-tuple-element.38.winds, f32[120,128]{1,0:T(8,128)S(1)} %collective-permute-done.2.west, f32[120,128]{1,0:T(8,128)S(1)} %collective-permute-done.3.east), custom_call_target="tpu_custom_call" | custom-call | flops 3795000064 | bytes 3300000 | tf_op jit(solution)/shard_map/weigh/pallas_call | solution.py:340
  40.7 4.4 %tangent.1.state = bf16[18,128,128]{2,1,0:T(8,128)(2,1)S(1)} custom-call(f32[16,128,128]{2,1,0:T(8,128)S(1)} %get-tuple-element.28.turned, f32[4,160,128]{2,1,0:T(8,128)S(1)} %collective-permute-done.south, f32[4,160,128]{2,1,0:T(8,128)S(1)} %collective-permute-done.1.north, f32[120,128]{1,0:T(8,128)S(1)} %collective-permute-done.2.west, ...), custom_call_target="tpu_custom_call" | custom-call | flops 5520000000 | bytes 4800000 | tf_op jit(solution)/shard_map/tangent/pallas_call | solution.py:374
  46.0 6.6 %all-to-all-done.got = bf16[128,4,640]{2,1,0:T(4,128)(2,1)S(1)} async-done(((bf16[128,4,640]{2,1,0:T(4,128)(2,1)}), bf16[128,4,640]{2,1,0:T(4,128)(2,1)S(1)}, u32[]{:S(2)}, u32[]{:S(2)}) %all-to-all-start) | async-done | bytes 655392 | tf_op jit(solution)/shard_map/all_to_all | solution.py:571
  52.6 1.1 %copy-done.12 = bf16[18,128,128]{2,1,0:T(8,128)(2,1)S(1)} copy-done((bf16[18,128,128]{2,1,0:T(8,128)(2,1)S(1)}, bf16[18,128,128]{2,1,0:T(8,128)(2,1)}, u32[]{:S(2)}) %copy-start.12) | copy-done | bytes 589848
  53.7 4.0 %scatter.1 = (f32[16,128,128]{2,1,0:T(8,128)S(1)}, bf16[4,128,128]{2,1,0:T(8,128)(2,1)S(1)}, bf16[4,128,128]{2,1,0:T(8,128)(2,1)}) custom-call(bf16[128,4,640]{2,1,0:T(4,128)(2,1)S(1)} %all-to-all-done.got, bf16[18,128,128]{2,1,0:T(8,128)(2,1)S(1)} %copy-done.12), custom_call_target="tpu_custom_call" | custom-call | flops 4255000064 | bytes 3700000 | tf_op jit(solution)/shard_map/scatter/pallas_call | solution.py:463
  57.7 1.2 %collective-permute-start.4 = (bf16[4,128,128]{2,1,0:T(8,128)(2,1)}, bf16[4,128,128]{2,1,0:T(8,128)(2,1)S(1)}, u32[]{:S(2)}, u32[]{:S(2)}) collective-permute-start(bf16[4,128,128]{2,1,0:T(8,128)(2,1)} %get-tuple-element.41), channel_id=1, source_target_pairs={{0,16},{16,32},{32,48},{48,64},{64,80},{80,96},{96,112},{112,0},{1... | collective-permute-start | bytes 393224 | tf_op jit(solution)/shard_map/ppermute | solution.py:567
  58.9 4.7 %gather.1 = bf16[128,2,1152]{2,1,0:T(2,128)(2,1)} custom-call(bf16[128,4,640]{2,1,0:T(4,128)(2,1)S(1)} %all-to-all-done.got, bf16[18,128,128]{2,1,0:T(8,128)(2,1)S(1)} %copy-done.13), custom_call_target="tpu_custom_call" | custom-call | flops 4485000192 | bytes 3900000 | tf_op jit(solution)/shard_map/gather/pallas_call | solution.py:427
  63.7 6.1 %all-to-all-start.1 = ((bf16[128,2,1152]{2,1,0:T(2,128)(2,1)}), bf16[128,2,1152]{2,1,0:T(2,128)(2,1)S(1)}, u32[]{:S(2)}, u32[]{:S(2)}) async-start(bf16[128,2,1152]{2,1,0:T(2,128)(2,1)} %gather.1), calls=%async_computation.1 | async-start | bytes 1179648 | tf_op jit(solution)/shard_map/all_to_all | solution.py:571
  69.8 1.5 %collective-permute-start.6 = (bf16[96,128]{1,0:T(8,128)(2,1)S(1)}, bf16[96,128]{1,0:T(8,128)(2,1)S(1)}, u32[]{:S(2)}, u32[]{:S(2)}) collective-permute-start(bf16[96,128]{1,0:T(8,128)(2,1)S(1)} %get-tuple-element.42), channel_id=1, source_target_pairs={{0,1},{1,2},{2,3},{3,4},{4,5},{5,6},{6,7},{7,8},{8,9},{9,10},{10,1... | collective-permute-start | bytes 73736 | tf_op jit(solution)/shard_map/ppermute | solution.py:567
  71.3 3.9 %collective-permute-start.7 = (bf16[96,128]{1,0:T(8,128)(2,1)S(1)}, bf16[96,128]{1,0:T(8,128)(2,1)S(1)}, u32[]{:S(2)}, u32[]{:S(2)}) collective-permute-start(bf16[96,128]{1,0:T(8,128)(2,1)S(1)} %get-tuple-element.43), channel_id=1, source_target_pairs={{0,15},{1,0},{2,1},{3,2},{4,3},{5,4},{6,5},{7,6},{8,7},{9,8},{10,9... | collective-permute-start | bytes 73736 | tf_op jit(solution)/shard_map/ppermute | solution.py:567
  75.9 0.8 copy-done.7
  76.8 3.3 %weigh.3.coefs = f32[24,24,5,8,128]{4,3,2,1,0:T(8,128)S(1)} custom-call(f32[6,128,128]{2,1,0:T(8,128)S(1)} %get-tuple-element.38.winds, f32[120,128]{1,0:T(8,128)S(1)} %copy-done.5, f32[120,128]{1,0:T(8,128)S(1)} %copy-done.7), custom_call_target="tpu_custom_call" | custom-call | flops 3795000064 | bytes 3300000 | tf_op jit(solution)/shard_map/weigh/pallas_call | solution.py:340
  80.1 1.4 %collective-permute-done.6.west = bf16[96,128]{1,0:T(8,128)(2,1)S(1)} collective-permute-done((bf16[96,128]{1,0:T(8,128)(2,1)S(1)}, bf16[96,128]{1,0:T(8,128)(2,1)S(1)}, u32[]{:S(2)}, u32[]{:S(2)}) %collective-permute-start.6) | collective-permute-done | bytes 24608 | tf_op jit(solution)/shard_map/ppermute | solution.py:567
  81.5 5.3 %adjoint.1 = f32[2048,128]{1,0:T(8,128)} custom-call(f32[2048,128]{1,0:T(8,128)S(1)} %bitcast.10, f32[24,24,5,8,128]{4,3,2,1,0:T(8,128)S(1)} %weigh.3.coefs, f32[16,128,128]{2,1,0:T(8,128)S(1)} %get-tuple-element.40.forcing, bf16[4,128,128]{2,1,0:T(8,128)(2,1)S(1)} %collective-permute-done.4.south, bf16[4,128,128]{2,1,0:T(8,128)(2,1)S(1)} %collective-permute-done.5.north, ...), custom_call_target="tpu_custom_call" | custom-call | flops 8049999872 | bytes 7000000 | tf_op jit(solution)/shard_map/adjoint/pallas_call | solution.py:525
  86.8 1.1 %copy-done.14 = bf16[300,1152]{1,0:T(8,128)(2,1)S(1)} copy-done((bf16[300,1152]{1,0:T(8,128)(2,1)S(1)}, bf16[300,1152]{1,0:T(8,128)(2,1)}, u32[]{:S(2)}) %copy-start.14) | copy-done | bytes 691224
  87.9 3.1 %depart.1 = bf16[300,1152]{1,0:T(8,128)(2,1)} custom-call(s32[1,1152]{1,0:T(1,128)S(1)} %bitcast.15, bf16[128,2,1152]{2,1,0:T(2,128)(2,1)S(1)} %all-to-all-done.1.back, bf16[300,1152]{1,0:T(8,128)(2,1)S(1)} %copy-done.14, bf16[300,128]{1,0:T(8,128)(2,1)S(1)} %bitcast.13, f32[300]{0:T(512)S(1)} %copy-done.10), custom_call_target="tpu_custom_call" | custom-call | flops 4024999936 | bytes 3500000 | tf_op jit(solution)/shard_map/depart/pallas_call | solution.py:557
  (38 shorter events, 1.9 us)
Async XLA Ops:
  3.6 7.8 %collective-permute-start = (f32[4,160,128]{2,1,0:T(8,128)S(1)}, f32[4,160,128]{2,1,0:T(8,128)S(1)}, u32[]{:S(2)}, u32[]{:S(2)}) collective-permute-start(f32[4,160,128]{2,1,0:T(8,128)S(1)} %get-tuple-element.24), channel_id=1, source_target_pairs={{0,16},{16,32},{32,48},{48,64},{64,80},{80,96},{96,112},{112,0},{1... | collective-permute-start | bytes 983048 | tf_op jit(solution)/shard_map/ppermute | solution.py:567
  6.7 6.5 %collective-permute-start.1 = (f32[4,160,128]{2,1,0:T(8,128)S(1)}, f32[4,160,128]{2,1,0:T(8,128)S(1)}, u32[]{:S(2)}, u32[]{:S(2)}) collective-permute-start(f32[4,160,128]{2,1,0:T(8,128)S(1)} %get-tuple-element.25), channel_id=1, source_target_pairs={{0,112},{16,0},{32,16},{48,32},{64,48},{80,64},{96,80},{112,96},{1... | collective-permute-start | bytes 983048 | tf_op jit(solution)/shard_map/ppermute | solution.py:567
  6.7 6.5 %copy-start = (f32[2,16,16,128]{3,2,1,0:T(8,128)S(1)}, f32[2,16,16,128]{3,2,1,0:T(8,128)}, u32[]{:S(2)}) copy-start(f32[2,16,16,128]{3,2,1,0:T(8,128)} %param.9) | copy-start | bytes 786436
  6.7 11.8 %copy-start.2 = (bf16[128,300]{0,1:T(8,128)(2,1)S(1)}, bf16[128,300]{0,1:T(8,128)(2,1)}, u32[]{:S(2)}) copy-start(bf16[128,300]{0,1:T(8,128)(2,1)} %param.12) | copy-start | bytes 230404
  6.7 11.8 %copy-start.8 = (s32[1152]{0:T(1024)S(1)}, s32[1152]{0:T(1024)}, u32[]{:S(2)}) copy-start(s32[1152]{0:T(1024)} %cell.1) | copy-start | bytes 13828
  6.7 11.8 %copy-start.9 = (s32[1152,1]{0,1:T(1,128)S(1)}, s32[1152,1]{0,1:T(1,128)}, u32[]{:S(2)}) copy-start(s32[1152,1]{0,1:T(1,128)} %param.14) | copy-start | bytes 13828
  6.7 11.8 %copy-start.10 = (f32[300]{0:T(512)S(1)}, f32[300]{0:T(512)}, u32[]{:S(2)}) copy-start(f32[300]{0:T(512)} %weight.5) | copy-start | bytes 3604
  13.4 17.9 %collective-permute-start.2 = (f32[120,128]{1,0:T(8,128)S(1)}, f32[120,128]{1,0:T(8,128)S(1)}, u32[]{:S(2)}, u32[]{:S(2)}) collective-permute-start(f32[120,128]{1,0:T(8,128)S(1)} %get-tuple-element.31), channel_id=1, source_target_pairs={{0,1},{1,2},{2,3},{3,4},{4,5},{5,6},{6,7},{7,8},{8,9},{9,10},{10,1... | collective-permute-start | bytes 184328 | tf_op jit(solution)/shard_map/ppermute | solution.py:567
  14.6 16.6 %collective-permute-start.3 = (f32[120,128]{1,0:T(8,128)S(1)}, f32[120,128]{1,0:T(8,128)S(1)}, u32[]{:S(2)}, u32[]{:S(2)}) collective-permute-start(f32[120,128]{1,0:T(8,128)S(1)} %get-tuple-element.32), channel_id=1, source_target_pairs={{0,15},{1,0},{2,1},{3,2},{4,3},{5,4},{6,5},{7,6},{8,7},{9,8},{10,9... | collective-permute-start | bytes 184328 | tf_op jit(solution)/shard_map/ppermute | solution.py:567
  31.2 13.9 %copy-start.4 = (f32[120,128]{1,0:T(8,128)}, f32[120,128]{1,0:T(8,128)S(1)}, u32[]{:S(2)}) copy-start(f32[120,128]{1,0:T(8,128)S(1)} %collective-permute-done.2.west) | copy-start | bytes 184324
  31.2 13.9 %copy-start.6 = (f32[120,128]{1,0:T(8,128)}, f32[120,128]{1,0:T(8,128)S(1)}, u32[]{:S(2)}) copy-start(f32[120,128]{1,0:T(8,128)S(1)} %collective-permute-done.3.east) | copy-start | bytes 184324
  31.2 21.4 %all-to-all-start = ((bf16[128,4,640]{2,1,0:T(4,128)(2,1)}), bf16[128,4,640]{2,1,0:T(4,128)(2,1)S(1)}, u32[]{:S(2)}, u32[]{:S(2)}) async-start(bf16[128,4,640]{2,1,0:T(4,128)(2,1)} %get-tuple-element.33), calls=%async_computation | async-start | bytes 1310720 | tf_op jit(solution)/shard_map/all_to_all | solution.py:571
  52.6 1.1 %copy-start.12 = (bf16[18,128,128]{2,1,0:T(8,128)(2,1)S(1)}, bf16[18,128,128]{2,1,0:T(8,128)(2,1)}, u32[]{:S(2)}) copy-start(bf16[18,128,128]{2,1,0:T(8,128)(2,1)} %copy-done.11) | copy-start | bytes 1769476
  53.7 5.2 %copy-start.13 = (bf16[18,128,128]{2,1,0:T(8,128)(2,1)S(1)}, bf16[18,128,128]{2,1,0:T(8,128)(2,1)}, u32[]{:S(2)}) copy-start(bf16[18,128,128]{2,1,0:T(8,128)(2,1)} %copy-done.11) | copy-start | bytes 1769476
  57.7 12.0 %collective-permute-start.4 = (bf16[4,128,128]{2,1,0:T(8,128)(2,1)}, bf16[4,128,128]{2,1,0:T(8,128)(2,1)S(1)}, u32[]{:S(2)}, u32[]{:S(2)}) collective-permute-start(bf16[4,128,128]{2,1,0:T(8,128)(2,1)} %get-tuple-element.41), channel_id=1, source_target_pairs={{0,16},{16,32},{32,48},{48,64},{64,80},{80,96},{96,112},{112,0},{1... | collective-permute-start | bytes 393224 | tf_op jit(solution)/shard_map/ppermute | solution.py:567
  58.9 10.8 %collective-permute-start.5 = (bf16[4,128,128]{2,1,0:T(8,128)(2,1)S(1)}, bf16[4,128,128]{2,1,0:T(8,128)(2,1)S(1)}, u32[]{:S(2)}, u32[]{:S(2)}) collective-permute-start(bf16[4,128,128]{2,1,0:T(8,128)(2,1)S(1)} %get-tuple-element.37), channel_id=1, source_target_pairs={{0,112},{16,0},{32,16},{48,32},{64,48},{80,64},{96,80},{112,96},{1... | collective-permute-start | bytes 393224 | tf_op jit(solution)/shard_map/ppermute | solution.py:567
  63.7 17.8 %copy-start.1 = (f32[8,16,16,128]{3,2,1,0:T(8,128)S(1)}, f32[8,16,16,128]{3,2,1,0:T(8,128)}, u32[]{:S(2)}) copy-start(f32[8,16,16,128]{3,2,1,0:T(8,128)} %param.8) | copy-start | bytes 3145732
  63.7 23.2 %all-to-all-start.1 = ((bf16[128,2,1152]{2,1,0:T(2,128)(2,1)}), bf16[128,2,1152]{2,1,0:T(2,128)(2,1)S(1)}, u32[]{:S(2)}, u32[]{:S(2)}) async-start(bf16[128,2,1152]{2,1,0:T(2,128)(2,1)} %gather.1), calls=%async_computation.1 | async-start | bytes 1179648 | tf_op jit(solution)/shard_map/all_to_all | solution.py:571
  69.8 11.7 %collective-permute-start.6 = (bf16[96,128]{1,0:T(8,128)(2,1)S(1)}, bf16[96,128]{1,0:T(8,128)(2,1)S(1)}, u32[]{:S(2)}, u32[]{:S(2)}) collective-permute-start(bf16[96,128]{1,0:T(8,128)(2,1)S(1)} %get-tuple-element.42), channel_id=1, source_target_pairs={{0,1},{1,2},{2,3},{3,4},{4,5},{5,6},{6,7},{7,8},{8,9},{9,10},{10,1... | collective-permute-start | bytes 73736 | tf_op jit(solution)/shard_map/ppermute | solution.py:567
  71.3 10.3 %collective-permute-start.7 = (bf16[96,128]{1,0:T(8,128)(2,1)S(1)}, bf16[96,128]{1,0:T(8,128)(2,1)S(1)}, u32[]{:S(2)}, u32[]{:S(2)}) collective-permute-start(bf16[96,128]{1,0:T(8,128)(2,1)S(1)} %get-tuple-element.43), channel_id=1, source_target_pairs={{0,15},{1,0},{2,1},{3,2},{4,3},{5,4},{6,5},{7,6},{8,7},{9,8},{10,9... | collective-permute-start | bytes 73736 | tf_op jit(solution)/shard_map/ppermute | solution.py:567
  75.1 0.8 copy-start.5
  75.9 0.8 copy-start.7
  80.1 6.7 %copy-start.3 = (bf16[128,300]{0,1:T(8,128)(2,1)S(1)}, bf16[128,300]{0,1:T(8,128)(2,1)}, u32[]{:S(2)}) copy-start(bf16[128,300]{0,1:T(8,128)(2,1)} %param.12) | copy-start | bytes 230404
  86.8 1.1 %copy-start.14 = (bf16[300,1152]{1,0:T(8,128)(2,1)S(1)}, bf16[300,1152]{1,0:T(8,128)(2,1)}, u32[]{:S(2)}) copy-start(bf16[300,1152]{1,0:T(8,128)(2,1)} %get-tuple-element.45.scores) | copy-start | bytes 2073604
  (1 other events, 0.8 us)
